TPU v7x, 32 devices: a whole 2x2x4 slice. The times are simulated.
32 devices in a mesh: px: 8 (over y, x, core), py: 4 (over z).
Axes of the slice: x: 2, y: 2, z: 4, core: 2. Of those that a mesh axis runs over, the one named last changes fastest.
Arguments:
- cotangent: float32 [64, 64, 128], P('px', 'py'), may hold values from -6 to 6
- fraction: float32 [3, 64, 64, 128], P(None, 'px', 'py'), may hold values from 0 to 0.999
- grid_base: int32 [3, 64, 64, 128], P(None, 'px', 'py'), may hold values from 0 to 255, as said below
- cell_count: int32 [64, 64], P('px', 'py'), may hold values from 32 to 128, as said below
- influence: float32 [256, 256, 256], P(('px', 'py')), as said below
Outputs:
- charge_gradient: float32 [64, 64, 128], P('px', 'py')
Inputs may be any that keep to these rules, and one draw needn't show every extreme that they name: grid_base[0] // 4 is the cell's first index and grid_base[1] // 4 its second; grid_base[2] lies in 0 to 255. `cell_count`: some cell is full. Positive and even: influence[kz, kx, ky] equals influence[-kz, -kx, -ky], wave numbers taken modulo 256, 256, 256.
All inputs are finite; a program needn't handle non-finite values.
Results may differ from a plain program's by a relative error of at most 0.0003.
Values sent between devices are 32-bit elements; how exact they have to be, the bound alone decides.
A program may use at most 128 MiB of HBM per device.

v0:
```python
import math

import jax
import jax.numpy as jnp
from jax import lax
from jax.sharding import PartitionSpec as P

NZ = 256
CELL = 4


exact_prec = lax.Precision.HIGHEST


def with_halo(block, sides, width):
    for axis, dim in sides:
        count = lax.axis_size(axis)
        forward = [(i, i + 1) for i in range(count - 1)]
        forward.append((count - 1, 0))
        backward = [(target, source) for source, target in forward]
        low = lax.ppermute(
            lax.slice_in_dim(block, block.shape[dim] - width, None, axis=dim), axis, forward
        )
        high = lax.ppermute(lax.slice_in_dim(block, 0, width, axis=dim), axis, backward)
        block = jnp.concatenate([low, block, high], axis=dim)
    return block


def spline_weights(fractions):
    nothing = jnp.zeros_like(fractions)
    values = [fractions, 1.0 - fractions]
    for degree in (3, 4, 5):
        updated = []
        for position in range(degree):
            upper_term = values[position] if position < degree - 1 else nothing
            lower_term = values[position - 1] if position >= 1 else nothing
            updated.append(
                ((fractions + position) * upper_term + (degree - fractions - position) * lower_term)
                / (degree - 1)
            )
        values = updated
    return jnp.stack(values)


def window_weights(offsets, weights):
    position = jnp.arange(8, dtype=jnp.int32)[:, None]
    selected = 4 + offsets[:, :, None, :] - position
    summed = jnp.zeros(selected.shape, jnp.float32)
    for degree in range(5):
        summed = summed + jnp.where(selected == degree, weights[degree][:, :, None, :], 0.0)
    return summed


def depth_weights(depth_base, weights):
    levels = jnp.arange(NZ, dtype=jnp.int32)[None, :, None]
    offsets = (levels - depth_base[:, None, :] + NZ // 2) % NZ - NZ // 2
    selected = 2 - offsets
    summed = jnp.zeros(selected.shape, jnp.float32)
    for degree in range(5):
        summed = summed + jnp.where(selected == degree, weights[degree][:, None, :], 0.0)
    return summed


def fold_rims(mesh_grid, axis_index):
    extent = mesh_grid.shape[axis_index]
    interior = lax.slice_in_dim(mesh_grid, 4, extent - 4, axis=axis_index)
    interior_size = extent - 8
    lower_rim = lax.slice_in_dim(mesh_grid, 0, 2, axis=axis_index)
    upper_rim = lax.slice_in_dim(mesh_grid, extent - 2, extent, axis=axis_index)
    return jnp.concatenate(
        [
            lax.slice_in_dim(interior, 0, 2, axis=axis_index) + lower_rim,
            lax.slice_in_dim(interior, 2, interior_size - 2, axis=axis_index),
            lax.slice_in_dim(interior, interior_size - 2, interior_size, axis=axis_index)
            + upper_rim,
        ],
        axis=axis_index,
    )


def cosine_sine(length):
    indices = jnp.arange(length, dtype=jnp.int32)
    phases = indices[:, None] * indices[None, :] % length
    angles = phases.astype(jnp.float32) * (2.0 * math.pi / length)
    return (jnp.cos(angles), jnp.sin(angles))


def complex_table(length, sign):
    cosine, sine_part = cosine_sine(length)
    turned = sign * sine_part
    return jnp.stack([jnp.stack([cosine, turned]), jnp.stack([-turned, cosine])])


def per_device(cotangent, fraction, grid_base, cell_count, influence):
    cells_x, cells_y, slot_count = cotangent.shape
    local_x = cells_x * CELL
    local_y = cells_y * CELL
    slot_ids = jnp.arange(slot_count, dtype=jnp.int32)
    occupied = slot_ids[None, None, :] < cell_count[:, :, None]
    charge = jnp.where(occupied, cotangent, jnp.zeros_like(cotangent))
    window_x = window_weights(grid_base[0] % CELL, spline_weights(fraction[0]))
    window_y = window_weights(grid_base[1] % CELL, spline_weights(fraction[1]))
    depth_rows = jnp.moveaxis(spline_weights(fraction[2]), 1, 0)

    def spread_row(row):
        charge_row, across_x, across_y, across_z, base_z = row
        depth_table_row = depth_weights(base_z, across_z)
        lifted = charge_row[:, None, None, :] * across_x[:, :, None, :] * across_y[:, None, :, :]
        patches = jnp.einsum("buvs,bzs->buvz", lifted, depth_table_row, precision=exact_prec)
        stripe = jnp.zeros((8, local_y + 4, NZ), jnp.float32)
        for which_half in (0, 1):
            quarter = patches[:, :, CELL * which_half : CELL * which_half + CELL]
            quarter = jnp.transpose(quarter, (1, 0, 2, 3))
            quarter = jnp.pad(quarter, ((0, 0), (which_half, 1 - which_half), (0, 0), (0, 0)))
            stripe = stripe + quarter.reshape(8, local_y + 4, NZ)
        return stripe

    stripes = lax.map(spread_row, (charge, window_x, window_y, depth_rows, grid_base[2]))
    upper_half = jnp.pad(stripes[:, :CELL], ((0, 1), (0, 0), (0, 0), (0, 0)))
    lower_half = jnp.pad(stripes[:, CELL:], ((1, 0), (0, 0), (0, 0), (0, 0)))
    extended = (upper_half + lower_half).reshape(local_x + 4, local_y + 4, NZ)
    with_rims = with_halo(extended, (("px", 0), ("py", 1)), 2)
    spread = fold_rims(fold_rims(with_rims, 0), 1)
    px_size = lax.axis_size("px")
    py_size = lax.axis_size("py")
    full_x = px_size * local_x
    full_y = py_size * local_y
    cosine_z, sine_z = cosine_sine(NZ)
    depth_table = jnp.stack([cosine_z, -sine_z])
    forward_z, inverse_z = (depth_table, depth_table)
    spectrum_z = jnp.einsum("xyz,ckz->ckxy", spread, forward_z, precision=exact_prec)
    forward_y = complex_table(full_y, 1.0)
    forward_x = complex_table(full_x, 1.0)
    inverse_y = complex_table(full_y, -1.0)
    inverse_x = complex_table(full_x, -1.0)
    mixed_grid = lax.all_to_all(
        lax.all_to_all(spectrum_z, "px", split_axis=1, concat_axis=2, tiled=True),
        "py",
        split_axis=1,
        concat_axis=3,
        tiled=True,
    )
    along_y = jnp.einsum("czxy,dcyk->dzxk", mixed_grid, forward_y, precision=exact_prec)
    full_spectrum = jnp.einsum("czxy,dcxk->dzky", along_y, forward_x, precision=exact_prec)
    scaled = full_spectrum * influence[None]
    back_y = jnp.einsum("czxy,dcyk->dzxk", scaled, inverse_y, precision=exact_prec)
    back_x = jnp.einsum("czxy,dcxk->dzky", back_y, inverse_x, precision=exact_prec)
    half_back = lax.all_to_all(back_x, "py", split_axis=3, concat_axis=1, tiled=True)
    returned = lax.all_to_all(half_back, "px", split_axis=2, concat_axis=1, tiled=True)
    potential = jnp.einsum("ckxy,ckz->xyz", returned, inverse_z, precision=exact_prec) * (
        1.0 / (NZ * full_x * full_y)
    )
    halo_potential = with_halo(potential, (("px", 0), ("py", 1)), 2)

    def gather_row(row):
        row_index, across_x, across_y, across_z, base_z = row
        depth_table_row = depth_weights(base_z, across_z)
        stripe = lax.dynamic_slice_in_dim(halo_potential, row_index * CELL, 8, 0)
        blocks = stripe.reshape(8, cells_y + 1, CELL, NZ)
        window = jnp.concatenate([blocks[:, :-1], blocks[:, 1:]], axis=2)
        partial_value = jnp.einsum("ubvz,bzs->buvs", window, depth_table_row, precision=exact_prec)
        return jnp.sum(
            partial_value * across_x[:, :, None, :] * across_y[:, None, :, :], axis=(1, 2)
        )

    row_ids = jnp.arange(cells_x, dtype=jnp.int32)
    gradient = lax.map(gather_row, (row_ids, window_x, window_y, depth_rows, grid_base[2]))
    return jnp.where(occupied, gradient, jnp.zeros_like(gradient))


def solution(mesh):
    placed = (
        P("px", "py", None),
        P(None, "px", "py", None),
        P(None, "px", "py", None),
        P("px", "py"),
        P(("px", "py"), None, None),
    )
    return jax.shard_map(
        per_device, mesh=mesh, in_specs=placed, out_specs=P("px", "py", None), check_vma=False
    )
```

profile of v0, /device:TPU:0, one launch (start us, length us, event | category | flops | bytes accessed | tf_op | source)
XLA Modules:
  0.0 652.4 jit_solution(7368748727658377857)
XLA Ops:
  8.9 45.9 %while.26 = (s32[]{:T(128)}, f32[8,8,68,256]{3,1,2,0:T(8,128)}, f32[8,16,128]{2,1,0:T(8,128)S(1)}, f32[8,16,8,128]{3,2,1,0:T(8,128)S(1)}, f32[8,16,8,128]{3,2,1,...) while((s32[]{:T(128)}, f32[8,8,68,256]{3,1,2,0:T(8,128)}, ...), condition=%wide.region_1.2_spmd.clone, body=%wide.region_0.1_spmd.sunk.clone | while | flops 418144256 | bytes 7545505 | solution.py:118
  9.0 4.2 fusion.250
  14.7 4.2 fusion.250
  20.5 4.2 fusion.250
  26.2 4.2 fusion.250
  32.0 4.2 fusion.250
  37.7 4.2 fusion.250
  43.4 4.2 fusion.250
  49.2 4.2 fusion.250
  54.8 4.6 fusion.230
  61.1 3.0 collective-permute-start.1
  64.0 2.8 collective-permute-done
  77.3 5.6 fusion.128
  82.9 9.2 %copy.55 = f32[2,256,32,64]{3,2,0,1:T(8,128)} copy(f32[2,256,32,64]{1,3,2,0:T(8,128)} %fusion.128) | data formatting | bytes 8388608 | tf_op jit(solution)/shard_map/xyz,ckz->ckxy/dot_general | solution.py:131
  92.1 9.8 %reshape.617 = f32[8,1,131072]{2,1,0:T(1,128)} reshape(f32[256,2,32,64]{3,2,1,0:T(8,128)} %bitcast.525) | data formatting | bytes 8388608
  101.9 53.6 %all_to_all.72 = f32[8,1,131072]{2,1,0:T(1,128)} all-to-all(f32[8,1,131072]{2,1,0:T(1,128)} %reshape.617), channel_id=1, replica_groups=mesh['px'=8,'py'=4] {'px'}, dimensions={0} | all-to-all | bytes 8388608 | tf_op jit(solution)/shard_map/all_to_all | solution.py:137
  156.0 13.7 %reduce = f32[8,131072]{1,0:T(8,128)} reduce(f32[8,1,131072]{2,1,0:T(1,128)} %all_to_all.72, f32[]{:T(128)} %broadcast.1295), dimensions={1}, to_apply=%all_to_all.52.reduce_sub_computation | reduce | bytes 8388612 | tf_op jit(solution)/shard_map/all_to_all | solution.py:137
  169.7 8.7 %reshape.618 = f32[256,2,32,64]{3,2,1,0:T(8,128)} reshape(f32[8,131072]{1,0:T(8,128)} %reduce) | data formatting | bytes 8388608
  178.4 8.0 %copy.57 = f32[2,32,8,32,64]{4,3,2,1,0:T(8,128)} copy(f32[2,32,8,32,64]{4,3,0,1,2:T(8,128)} %bitcast.528) | data formatting | bytes 8388608 | tf_op jit(solution)/shard_map/all_to_all | solution.py:137
  186.5 6.8 %copy.58 = f32[2,32,256,64]{2,3,0,1:T(8,128)} copy(f32[2,32,256,64]{3,2,1,0:T(8,128)} %bitcast.529) | data formatting | bytes 8388608 | tf_op jit(solution)/shard_map/all_to_all | solution.py:137
  193.2 5.3 all-to-all-start.1
  200.7 90.3 %all-to-all-done.1 = f32[2,32,256,64]{2,3,0,1:T(8,128)} async-done(((f32[2,32,256,64]{2,3,0,1:T(8,128)}), f32[2,32,256,64]{2,3,0,1:T(8,128)}, u32[]{:S(2)}, u32[]{:S(2)}) %all-to-all-start.1) | async-done | bytes 4194336 | tf_op jit(solution)/shard_map/all_to_all | solution.py:136
  293.4 7.5 %fusion.135 = f32[2,256,8,256,1]{3,1,2,4,0:T(8,128)S(1)} fusion(f32[2,8,256,256,1]{2,3,1,0,4:T(8,128)S(1)} %bitcast.532, f32[1,2,256,256]{3,2,1,0:T(8,128)S(1)} %get-tuple-element.285, f32[1,2,256,256]{3,2,1,0:T(8,128)S(1)} %get-tuple-element.286), kind=kOutput, calls=%fused_computation.157 | convolution fusion | flops 6442713088 | bytes 9437184 | tf_op jit(solution)/shard_map/czxy,dcyk->dzxk/dot_general | solution.py:143
  300.9 14.0 %fusion.116 = f32[2,8,256,256,1]{3,2,1,0,4:T(8,128)S(1)} fusion(f32[2,256,8,256,1]{3,1,2,4,0:T(8,128)S(1)} %fusion.135, f32[8,256,256]{2,1,0:T(8,128)S(1)} %copy-done, f32[1,2,256,256]{3,2,1,0:T(8,128)S(1)} %get-tuple-element.285, f32[1,2,256,256]{3,2,1,0:T(8,128)S(1)} %get-tuple-element.286), kind=kOutput, calls=%fused_computation.138 | convolution fusion | flops 6443761664 | bytes 11534336 | tf_op jit(solution)/shard_map/czxy,dcxk->dzky/dot_general | solution.py:144
  314.9 14.0 %fusion.121 = f32[2,256,8,256,1]{3,1,4,0,2:T(8,128)S(1)} fusion(f32[2,8,256,256,1]{3,2,1,0,4:T(8,128)S(1)} %fusion.116, f32[1,2,256,256]{3,2,1,0:T(8,128)S(1)} %get-tuple-element.287, f32[1,2,256,256]{3,2,1,0:T(8,128)S(1)} %get-tuple-element.284), kind=kOutput, calls=%fused_computation.143 | convolution fusion | flops 6442713088 | bytes 9437184 | tf_op jit(solution)/shard_map/czxy,dcyk->dzxk/dot_general | solution.py:146
  328.9 15.2 %fusion.123 = f32[2,8,256,256]{3,2,1,0:T(8,128)} fusion(f32[2,256,8,256,1]{3,1,4,0,2:T(8,128)S(1)} %fusion.121, f32[1,2,256,256]{3,2,1,0:T(8,128)S(1)} %get-tuple-element.287, f32[1,2,256,256]{3,2,1,0:T(8,128)S(1)} %get-tuple-element.284), kind=kOutput, calls=%fused_computation.149 | convolution fusion | flops 6442713088 | bytes 9437184 | tf_op jit(solution)/shard_map/czxy,dcxk->dzky/dot_general | solution.py:147
  344.1 5.5 copy.69
  349.6 96.6 %all_to_all.73 = f32[2,8,256,256]{2,1,0,3:T(8,128)S(1)} all-to-all(f32[2,8,256,256]{2,1,0,3:T(8,128)} %copy.69), channel_id=1, replica_groups=mesh['px'=8,'py'=4] {'py'}, dimensions={3} | all-to-all | bytes 8388608 | tf_op jit(solution)/shard_map/all_to_all | solution.py:148
  446.2 4.4 copy.71
  450.6 9.2 %copy.72 = f32[2,32,256,64]{3,1,0,2:T(8,128)} copy(f32[2,32,256,64]{2,3,1,0:T(8,128)} %bitcast.531) | data formatting | bytes 8388608 | tf_op jit(solution)/shard_map/all_to_all | solution.py:148
  459.8 9.8 %reshape.619 = f32[8,1,131072]{2,1,0:T(1,128)} reshape(f32[256,2,32,64]{3,2,1,0:T(8,128)} %bitcast.526) | data formatting | bytes 8388608
  469.6 53.6 %all_to_all.74 = f32[8,1,131072]{2,1,0:T(1,128)} all-to-all(f32[8,1,131072]{2,1,0:T(1,128)} %reshape.619), channel_id=1, replica_groups=mesh['px'=8,'py'=4] {'px'}, dimensions={0} | all-to-all | bytes 8388608 | tf_op jit(solution)/shard_map/all_to_all | solution.py:149
  523.2 14.1 %reduce.1 = f32[8,131072]{1,0:T(8,128)} reduce(f32[8,1,131072]{2,1,0:T(1,128)} %all_to_all.74, f32[]{:T(128)} %broadcast.1295), dimensions={1}, to_apply=%all_to_all.64.reduce_sub_computation | reduce | bytes 8388612 | tf_op jit(solution)/shard_map/all_to_all | solution.py:149
  537.3 8.7 %reshape.620 = f32[256,2,32,64]{3,2,1,0:T(8,128)} reshape(f32[8,131072]{1,0:T(8,128)} %reduce.1) | data formatting | bytes 8388608
  546.0 9.9 %copy.74 = f32[2,8,32,32,64]{4,3,2,1,0:T(8,128)S(1)} copy(f32[2,8,32,32,64]{4,2,0,3,1:T(8,128)} %bitcast.530) | data formatting | bytes 8388608 | tf_op jit(solution)/shard_map/all_to_all | solution.py:149
  555.9 16.9 %bitcast_multiply_fusion.2 = f32[32,64,256]{2,1,0:T(8,128)S(1)} fusion(f32[2,256,32,64]{3,2,1,0:T(8,128)S(1)} %bitcast.527, f32[1,256,256]{2,1,0:T(8,128)S(1)} %get-tuple-element.302, f32[1,256,256]{2,1,0:T(8,128)S(1)} %get-tuple-element.303), kind=kOutput, calls=%fused_computation.156 | convolution fusion | flops 3221880832 | bytes 6815744 | tf_op jit(solution)/shard_map/ckxy,ckz->xyz/dot_general | solution.py:150
  572.9 2.6 collective-permute-start.5
  575.5 4.0 collective-permute-done.4
  579.9 3.6 collective-permute-start.7
  589.4 62.1 %while.27 = (s32[]{:T(128)}, f32[8,16,128]{2,1,0:T(8,128)S(1)}, s32[8]{0:T(128)S(1)}, f32[36,68,256]{2,0,1:T(8,128)}, s32[8,16,128]{2,1,0:T(8,128)S(1)}, /*index...) while((s32[]{:T(128)}, f32[8,16,128]{2,1,0:T(8,128)S(1)}, ...), condition=%wide.region_4.5_spmd.clone, body=%wide.region_2.4_spmd.sunk.clone | while | flops 418510848 | bytes 6922475 | solution.py:167
  593.4 3.7 fusion.254
  601.2 3.7 fusion.254
  608.9 3.7 fusion.254
  616.7 3.7 fusion.254
  624.5 3.7 fusion.254
  632.2 3.7 fusion.254
  640.0 3.7 fusion.254
  647.7 3.7 fusion.254
  (198 shorter events, 71.4 us)
Async XLA Ops:
  54.8 4.7 copy-start.1
  60.6 6.2 collective-permute-start
  61.1 6.2 collective-permute-start.1
  67.3 6.6 %collective-permute-start.2 = (f32[40,2,256]{2,1,0:T(2,128)S(1)}, f32[40,2,256]{2,1,0:T(2,128)S(1)}, u32[]{:S(2)}, u32[]{:S(2)}) collective-permute-start(f32[40,2,256]{2,1,0:T(2,128)S(1)} %get-tuple-element.274), channel_id=1, source_target_pairs={{0,1},{1,2},{2,3},{3,0},{4,5},{5,6},{6,7},{7,4},{8,9},{9,10},{10,1... | collective-permute-start | bytes 245768 | tf_op jit(solution)/shard_map/ppermute | solution.py:21
  69.2 7.1 %collective-permute-start.3 = (f32[40,2,256]{2,1,0:T(2,128)S(1)}, f32[40,2,256]{2,1,0:T(2,128)S(1)}, u32[]{:S(2)}, u32[]{:S(2)}) collective-permute-start(f32[40,2,256]{2,1,0:T(2,128)S(1)} %get-tuple-element.275), channel_id=1, source_target_pairs={{1,0},{2,1},{3,2},{0,3},{5,4},{6,5},{7,6},{4,7},{9,8},{10,9},{11,1... | collective-permute-start | bytes 245768 | tf_op jit(solution)/shard_map/ppermute | solution.py:24
  193.2 97.7 %all-to-all-start.1 = ((f32[2,32,256,64]{2,3,0,1:T(8,128)}), f32[2,32,256,64]{2,3,0,1:T(8,128)}, u32[]{:S(2)}, u32[]{:S(2)}) async-start(f32[2,32,256,64]{2,3,0,1:T(8,128)} %copy.58), calls=%async_computation.1 | async-start | bytes 8388608 | tf_op jit(solution)/shard_map/all_to_all | solution.py:136
  293.4 7.5 %copy-start = (f32[8,256,256]{2,1,0:T(8,128)S(1)}, f32[8,256,256]{2,1,0:T(8,128)}, u32[]{:S(2)}) copy-start(f32[8,256,256]{2,1,0:T(8,128)} %param.13) | copy-start | bytes 6291460
  572.8 6.7 %collective-permute-start.4 = (f32[2,64,256]{2,1,0:T(8,128)S(1)}, f32[2,64,256]{2,1,0:T(8,128)S(1)}, u32[]{:S(2)}, u32[]{:S(2)}) collective-permute-start(f32[2,64,256]{2,1,0:T(8,128)S(1)} %get-tuple-element.282), channel_id=1, source_target_pairs={{0,4},{4,8},{8,12},{12,16},{16,20},{20,24},{24,28},{28,0},{1,5},{5... | collective-permute-start | bytes 393224 | tf_op jit(solution)/shard_map/ppermute | solution.py:21
  572.9 6.6 %collective-permute-start.5 = (f32[2,64,256]{2,1,0:T(8,128)S(1)}, f32[2,64,256]{2,1,0:T(8,128)S(1)}, u32[]{:S(2)}, u32[]{:S(2)}) collective-permute-start(f32[2,64,256]{2,1,0:T(8,128)S(1)} %get-tuple-element.283), channel_id=1, source_target_pairs={{4,0},{8,4},{12,8},{16,12},{20,16},{24,20},{28,24},{0,28},{5,1},{9... | collective-permute-start | bytes 393224 | tf_op jit(solution)/shard_map/ppermute | solution.py:24
  579.6 6.2 collective-permute-start.6
  579.9 5.9 collective-permute-start.7
  587.0 2.4 copy-start.2
  589.4 62.1 %copy-start.3 = (s32[8,16]{1,0:T(8,128)S(1)}, s32[8,16]{1,0:T(8,128)}, u32[]{:S(2)}) copy-start(s32[8,16]{1,0:T(8,128)} %param.12) | copy-start | bytes 1540
where the time goes:
time: 661 us; the launch traced here: 652 us
  blocking collectives  204 us (31%)
  local copies, waits for them, and re-layouts  139 us (21%)
  matrix products  136 us (21%)
  waiting for transfers between devices  104 us (16%)
  other arithmetic  43.8 us (7%)
  starting transfers between devices  19.5 us (3%)
    all_to_all x1, blocking collectives, per_device(): lax.all_to_all(back_x, 'py', split_axis=3, concat_axis=1, tiled=True)  96.6 us
    all_to_all x1, waiting for transfers between devices, per_device(): lax.all_to_all(lax.all_to_all(spectrum_z, 'px', split_axis=1, concat_axis...  90.3 us
    all_to_all x1, blocking collectives, per_device(): lax.all_to_all(spectrum_z, 'px', split_axis=1, concat_axis=2, tiled=True)  53.6 us
    all_to_all x1, blocking collectives, per_device(): lax.all_to_all(half_back, 'px', split_axis=2, concat_axis=1, tiled=True)  53.6 us
    unnamed x12, local copies, waits for them, and re-layouts  37.1 us
    dot_general x8, matrix products, spread_row(): jnp.einsum('buvs,bzs->buvz', lifted, depth_table_row, precision=exact_prec)  33.9 us
    dot_general x8, matrix products, gather_row(): jnp.einsum('ubvz,bzs->buvs', window, depth_table_row, precision=exact_prec)  29.4 us
    dot_general x1, matrix products, per_device(): jnp.einsum('ckxy,ckz->xyz', returned, inverse_z, precision=exact_prec)  16.9 us
  transfers between devices with their start and end apart: 9, of which 7 were waited for; matrix products, arithmetic and copies ran while one was open for 0% of the time, Pallas kernels for 0%

commit v1 on v0

v1 whole, which is shorter than its diff:
```python
import functools
import math

import jax
import jax.numpy as jnp
import ml_dtypes
import numpy as np
from jax import lax
from jax.experimental import pallas as pl
from jax.experimental.pallas import tpu as pltpu
from jax.sharding import PartitionSpec as P

CELL = 4
REACH = 8
VMEM_LIMIT = 48 * 1024 * 1024


def halves_np(table):
    high = np.asarray(table, np.float32).astype(ml_dtypes.bfloat16)
    low = (np.asarray(table, np.float64) - high.astype(np.float64)).astype(ml_dtypes.bfloat16)
    return jnp.asarray(np.stack([high, low]))


def halves(value):
    high = value.astype(jnp.bfloat16)
    low = (value - high.astype(jnp.float32)).astype(jnp.bfloat16)
    return high, low


def dot3(left, right, dims):
    def one(a, b):
        return lax.dot_general(a, b, (dims, ((), ())), preferred_element_type=jnp.float32)

    return one(left[0], right[0]) + (one(left[0], right[1]) + one(left[1], right[0]))


NN = ((1,), (0,))
NT = ((1,), (1,))


def spline_weights(fractions):
    values = [fractions, 1.0 - fractions]
    for degree in (3, 4, 5):
        updated = []
        for position in range(degree):
            term = None
            if position < degree - 1:
                term = (fractions + position) * values[position]
            if position >= 1:
                lower = (degree - fractions - position) * values[position - 1]
                term = lower if term is None else term + lower
            updated.append(term * (1.0 / (degree - 1)))
        values = updated
    return values


def window_weights(offset, weights):
    position = lax.broadcasted_iota(jnp.int32, (REACH, offset.shape[1]), 0)
    selected = 4 + offset - position
    total = jnp.zeros(selected.shape, jnp.float32)
    for degree in range(5):
        total = jnp.where(selected == degree, weights[degree], total)
    return total


def depth_weights(base, weights, size):
    level = lax.broadcasted_iota(jnp.int32, (size, base.shape[1]), 0)
    selected = (base + 2 - level) & (size - 1)
    total = jnp.zeros(selected.shape, jnp.float32)
    for degree in range(5):
        total = jnp.where(selected == degree, weights[degree], total)
    return total


def cell_tables(across, base_ref, cell, size):
    def row(values):
        return [value[cell : cell + 1, :] for value in values]

    window_x = window_weights(base_ref[0, 0, cell : cell + 1, :] & (CELL - 1), row(across[0]))
    window_y = window_weights(base_ref[1, 0, cell : cell + 1, :] & (CELL - 1), row(across[1]))
    depth = depth_weights(base_ref[2, 0, cell : cell + 1, :], row(across[2]), size)
    return window_x, window_y, halves(depth)


def spread_kernel(size, charge_ref, fraction_ref, base_ref, out_ref):
    row = pl.program_id(0)

    @pl.when(row == 0)
    def _():
        out_ref[...] = jnp.zeros_like(out_ref)

    across = [spline_weights(fraction_ref[dim, 0]) for dim in range(3)]
    charge = charge_ref[0]
    cells_y, slots = charge.shape
    for cell in range(cells_y):
        window_x, window_y, depth = cell_tables(across, base_ref, cell, size)
        loaded = charge[cell : cell + 1, :] * window_x
        lifted = (loaded[:, None, :] * window_y[None, :, :]).reshape(REACH * REACH, slots)
        patch = dot3(halves(lifted), depth, NT).reshape(REACH, REACH, size)
        span = (pl.ds(row * CELL, REACH), pl.ds(cell * CELL, REACH), slice(None))
        out_ref[span] = out_ref[span] + patch


def gather_kernel(size, fraction_ref, base_ref, grid_ref, out_ref):
    row = pl.program_id(0)
    across = [spline_weights(fraction_ref[dim, 0]) for dim in range(3)]
    cells_y, slots = fraction_ref.shape[2:]
    for cell in range(cells_y):
        window_x, window_y, depth = cell_tables(across, base_ref, cell, size)
        span = (pl.ds(row * CELL, REACH), pl.ds(cell * CELL, REACH), slice(None))
        window = grid_ref[span].reshape(REACH * REACH, size)
        value = dot3(halves(window), depth, NN).reshape(REACH, REACH, slots)
        value = jnp.sum(value * window_x[:, None, :], axis=0) * window_y
        out_ref[0, cell : cell + 1, :] = jnp.sum(value, axis=0, keepdims=True)


def depth_forward_kernel(grid_ref, table_ref, out_ref):
    extent_x, extent_y, size = grid_ref.shape
    pairs = extent_x // 2
    table = (table_ref[0], table_ref[1])
    for pair in range(pairs):
        block = grid_ref[2 * pair : 2 * pair + 2].reshape(2 * extent_y, size)
        out_ref[pl.ds(pair, size, stride=pairs), :] = dot3(table, halves(block), NT)


def depth_inverse_kernel(in_ref, table_ref, out_ref):
    extent_x, extent_y, size = out_ref.shape
    pairs = extent_x // 2
    table = (table_ref[0], table_ref[1])
    for pair in range(pairs):
        block = in_ref[pl.ds(pair, size, stride=pairs), :].T
        out_ref[2 * pair : 2 * pair + 2] = dot3(halves(block), table, NN).reshape(
            2, extent_y, size
        )


def plane_kernel(
    start_ref, in_ref, own_ref, other_ref, right_ref, back_ref, left_ref, left_back_ref, out_ref
):
    count_x, count_y, parts, pairs, lanes = in_ref.shape
    half = lanes // 2
    rows = count_x * pairs
    full_y = count_y * half
    full_x = 2 * rows
    right = (right_ref[0], right_ref[1])
    back = (back_ref[0], back_ref[1])
    left = (left_ref[0], left_ref[1])
    left_back = (left_back_ref[0], left_back_ref[1])

    def load(part):
        blocks = [in_ref[:, y, part].reshape(rows, lanes) for y in range(count_y)]
        top = jnp.concatenate([block[:, :half] for block in blocks], axis=1)
        bottom = jnp.concatenate([block[:, half:] for block in blocks], axis=1)
        return jnp.concatenate([top, bottom], axis=0)

    def along_x(table, real, imag):
        both = dot3(table, halves(jnp.concatenate([real, imag], axis=1)), NN)
        upper, lower = both[:full_x], both[full_x:]
        return (
            upper[:, :full_y] - lower[:, full_y:],
            upper[:, full_y:] + lower[:, :full_y],
        )

    first = dot3(halves(load(0)), right, NN)
    second = dot3(halves(load(1)), right, NN)
    first = (first[:, :full_y], first[:, full_y:])
    second = (second[:, :full_y], second[:, full_y:])

    def finish(real, imag):
        real, imag = along_x(left_back, real, imag)
        both = dot3(halves(jnp.concatenate([real, imag], axis=0)), back, NN)
        upper, lower = both[:full_x], both[full_x:]
        results = (
            upper[:, :full_y] - lower[:, full_y:],
            upper[:, full_y:] + lower[:, :full_y],
        )
        for part in range(2):
            result = results[part]
            for y in range(count_y):
                columns = slice(y * half, (y + 1) * half)
                block = jnp.concatenate(
                    [result[:rows, columns], result[rows:, columns]], axis=1
                )
                out_ref[:, y, part] = block.reshape(count_x, pairs, lanes)

    own = own_ref[0]

    @pl.when(pl.program_id(0) == 0)
    def _():
        other = other_ref[0]
        ar, ai = along_x(left, *first)
        br, bi = along_x(left, *second)
        finish(own * ar - other * bi, own * ai + other * br)

    @pl.when(pl.program_id(0) != 0)
    def _():
        real, imag = along_x(left, first[0] - second[1], first[1] + second[0])
        finish(own * real, own * imag)


def with_halo(block, sides, width):
    for axis, dim in sides:
        count = lax.axis_size(axis)
        forward = [(i, (i + 1) % count) for i in range(count)]
        backward = [(target, source) for source, target in forward]
        low = lax.ppermute(
            lax.slice_in_dim(block, block.shape[dim] - width, None, axis=dim), axis, forward
        )
        high = lax.ppermute(lax.slice_in_dim(block, 0, width, axis=dim), axis, backward)
        block = jnp.concatenate([low, block, high], axis=dim)
    return block


def fold_halo(block, sides, width):
    for axis, dim in sides:
        count = lax.axis_size(axis)
        extent = block.shape[dim]
        forward = [(i, (i + 1) % count) for i in range(count)]
        backward = [(target, source) for source, target in forward]
        low = lax.ppermute(
            lax.slice_in_dim(block, extent - width, None, axis=dim), axis, forward
        )
        high = lax.ppermute(lax.slice_in_dim(block, 0, width, axis=dim), axis, backward)

        def part(start, stop):
            return lax.slice_in_dim(block, start, stop, axis=dim)

        block = jnp.concatenate(
            [
                part(width, 2 * width) + low,
                part(2 * width, extent - 2 * width),
                part(extent - 2 * width, extent - width) + high,
            ],
            axis=dim,
        )
    return block


def wave_tables(size, devices, scale):
    each = size // devices
    rows, weights = [], []
    points = np.arange(size)
    for device in range(devices):
        for plane in range(each // 2):
            wave = device * each + plane + (0 if device < devices // 2 else 1)
            angle = (wave * points % size) * (2.0 * math.pi / size)
            if wave == 0:
                rows += [np.ones(size), 1.0 - 2.0 * (points % 2)]
                weights += [1.0, 1.0]
            else:
                rows += [np.cos(angle), -np.sin(angle)]
                weights += [2.0, 2.0]
    forward = np.stack(rows)
    return forward, forward * (np.array(weights)[:, None] * scale)


def angles(first, second, size):
    return (first[:, None] * second[None, :] % size) * (2.0 * math.pi / size)


def per_device(cotangent, fraction, grid_base, cell_count, influence):
    cells_x, cells_y, slots = cotangent.shape
    full_x, full_y = influence.shape[1:]
    px_size = lax.axis_size("px")
    py_size = lax.axis_size("py")
    devices = px_size * py_size
    each = influence.shape[0]
    size = each * devices
    planes = each // 2
    local_x = cells_x * CELL
    local_y = cells_y * CELL
    pairs = local_x // 2
    lanes = 2 * local_y
    params = pltpu.CompilerParams(vmem_limit_bytes=VMEM_LIMIT)
    device = lax.axis_index("px") * py_size + lax.axis_index("py")

    occupied = jnp.arange(slots, dtype=jnp.int32)[None, None, :] < cell_count[:, :, None]
    charge = jnp.where(occupied, cotangent, 0.0)

    extra = lax.ppermute(influence[:1], ("px", "py"), [(devices // 2, 0)])
    start = jnp.where(device < devices // 2, 0, 1).astype(jnp.int32)
    own_first = lax.dynamic_slice_in_dim(influence, start, 1, axis=0)
    other = jnp.where(device == 0, extra, own_first)

    whole = lambda *dims: pl.BlockSpec(dims, lambda *_: (0,) * len(dims))
    atoms = pl.BlockSpec((3, 1, cells_y, slots), lambda i: (0, i, 0, 0))
    cells = pl.BlockSpec((1, cells_y, slots), lambda i: (i, 0, 0))

    extended = pl.pallas_call(
        functools.partial(spread_kernel, size),
        grid=(cells_x,),
        in_specs=[cells, atoms, atoms],
        out_specs=whole(local_x + 4, local_y + 4, size),
        out_shape=jax.ShapeDtypeStruct((local_x + 4, local_y + 4, size), jnp.float32),
        compiler_params=params,
        name="spread",
    )(charge, fraction, grid_base)
    spread = fold_halo(extended, (("px", 0), ("py", 1)), 2)

    forward_z, inverse_z = wave_tables(size, devices, 1.0 / (size * full_x * full_y))
    columns = pl.pallas_call(
        depth_forward_kernel,
        out_shape=jax.ShapeDtypeStruct((size * pairs, lanes), jnp.float32),
        compiler_params=params,
        name="depth_forward",
    )(spread, halves_np(forward_z))
    mixed = lax.all_to_all(columns, ("px", "py"), split_axis=0, concat_axis=0, tiled=True)
    mixed = mixed.reshape(px_size, py_size, 2 * planes, pairs, lanes)

    order = np.arange(full_x).reshape(full_x // 2, 2).T.reshape(-1)
    y_angles = angles(np.arange(full_y), np.arange(full_y), full_y)
    x_angles = angles(np.arange(full_x), order, full_x)
    right = np.concatenate([np.cos(y_angles), -np.sin(y_angles)], axis=1)
    back = np.concatenate([np.cos(y_angles), np.sin(y_angles)], axis=1)
    left = np.concatenate([np.cos(x_angles), -np.sin(x_angles)], axis=0)
    left_back = np.concatenate([np.cos(x_angles.T), np.sin(x_angles.T)], axis=0)
    block = pl.BlockSpec(
        (px_size, py_size, 2, pairs, lanes), lambda i, start: (0, 0, i, 0, 0)
    )
    turned = pl.pallas_call(
        plane_kernel,
        grid_spec=pltpu.PrefetchScalarGridSpec(
            num_scalar_prefetch=1,
            grid=(planes,),
            in_specs=[
                block,
                pl.BlockSpec((1, full_x, full_y), lambda i, start: (i + start[0], 0, 0)),
                whole(1, full_x, full_y),
                whole(2, full_y, 2 * full_y),
                whole(2, full_y, 2 * full_y),
                whole(2, 2 * full_x, full_x),
                whole(2, 2 * full_x, full_x),
            ],
            out_specs=block,
        ),
        out_shape=jax.ShapeDtypeStruct(mixed.shape, jnp.float32),
        compiler_params=params,
        name="planes",
    )(
        start[None],
        mixed,
        influence,
        other,
        halves_np(right),
        halves_np(back),
        halves_np(left),
        halves_np(left_back),
    )
    returned = lax.all_to_all(
        turned.reshape(size * pairs, lanes), ("px", "py"), split_axis=0, concat_axis=0, tiled=True
    )
    potential = pl.pallas_call(
        depth_inverse_kernel,
        out_shape=jax.ShapeDtypeStruct((local_x, local_y, size), jnp.float32),
        compiler_params=params,
        name="depth_inverse",
    )(returned, halves_np(inverse_z))
    halo_potential = with_halo(potential, (("px", 0), ("py", 1)), 2)
    gradient = pl.pallas_call(
        functools.partial(gather_kernel, size),
        grid=(cells_x,),
        in_specs=[atoms, atoms, whole(local_x + 4, local_y + 4, size)],
        out_specs=cells,
        out_shape=jax.ShapeDtypeStruct(cotangent.shape, jnp.float32),
        compiler_params=params,
        name="gather",
    )(fraction, grid_base, halo_potential)
    return jnp.where(occupied, gradient, 0.0)


def solution(mesh):
    placed = (
        P("px", "py", None),
        P(None, "px", "py", None),
        P(None, "px", "py", None),
        P("px", "py"),
        P(("px", "py"), None, None),
    )
    return jax.shard_map(
        per_device, mesh=mesh, in_specs=placed, out_specs=P("px", "py", None), check_vma=False
    )
```

time: 661 us -> 192 us (0.29); the launches traced: 652 us -> 192 us
  blocking collectives: 204 us -> 51.5 us
  matrix products: 136 us -> 0 us
  local copies, waits for them, and re-layouts: 139 us -> 3.98 us
  Pallas kernels: 0 us -> 47.6 us
  other arithmetic: 43.8 us -> 3.59 us
  waiting for transfers between devices: 104 us -> 66 us
    all_to_all x3 -> x1, blocking collectives: 204 us -> 51.5 us  [per_device(): lax.all_to_all(turned.reshape(size * pairs, lanes), ('px', 'py'), split_a...]
    dot_general x22 -> x0, matrix products: 136 us -> none  [the longest x8 33.9 us: spread_row(): jnp.einsum('buvs,bzs->buvz', lifted, depth_table_row, precision=exact_prec)]
    all_to_all x1, waiting for transfers between devices: 90.3 us -> 25.3 us  [per_device(): lax.all_to_all(columns, ('px', 'py'), split_axis=0, concat_axis=0, tiled=...]
    pallas_call x0 -> x5, Pallas kernels: none -> 47.6 us  [the longest x1 14.7 us: per_device(): pl.pallas_call(plane_kernel, grid_spec=pltpu.PrefetchScalarGridSpec(num_s...]
    all_to_all x7 -> x0, local copies, waits for them, and re-layouts: 41.3 us -> none  [the longest x3 15.3 us: per_device(): lax.all_to_all(spectrum_z, 'px', split_axis=1, concat_axis=2, tiled=True)]
    unnamed x12 -> x22, local copies, waits for them, and re-layouts: 37.1 us -> 2.56 us
    ppermute x0 -> x5, waiting for transfers between devices: none -> 33.8 us  [the longest x1 19 us: per_device(): extra = lax.ppermute(influence[:1], ('px', 'py'), [(devices // 2, 0)])]
    all_to_all x2 -> x0, other arithmetic: 27.9 us -> none  [the longest x1 14.1 us: per_device(): lax.all_to_all(half_back, 'px', split_axis=2, concat_axis=1, tiled=True)]
  transfers between devices with their start and end apart: 9 -> 10, of which waited for: 7 -> 9; matrix products, arithmetic and copies ran while one was open for 0% -> 1% of each run, Pallas kernels for 0% -> 0%
where the time goes in v1:
time: 192 us
  waiting for transfers between devices  66 us (34%)
  blocking collectives  51.5 us (27%)
  Pallas kernels  47.6 us (25%)
  starting transfers between devices  18.9 us (10%)
  local copies, waits for them, and re-layouts  3.98 us (2%)
  other arithmetic  3.59 us (2%)
    all_to_all x1, blocking collectives, per_device(): lax.all_to_all(turned.reshape(size * pairs, lanes), ('px', 'py'), split_a...  51.5 us
    all_to_all x1, waiting for transfers between devices, per_device(): lax.all_to_all(columns, ('px', 'py'), split_axis=0, concat_axis=0, tiled=...  25.3 us
    ppermute x1, waiting for transfers between devices, per_device(): extra = lax.ppermute(influence[:1], ('px', 'py'), [(devices // 2, 0)])  19 us
    pallas_call x1, Pallas kernels, per_device(): pl.pallas_call(plane_kernel, grid_spec=pltpu.PrefetchScalarGridSpec(num_s...  14.7 us
    pallas_call x1, Pallas kernels, per_device(): pl.pallas_call(functools.partial(spread_kernel, size), grid=(cells_x,), i...  14.4 us
    pallas_call x1, Pallas kernels, per_device(): pl.pallas_call(functools.partial(gather_kernel, size), grid=(cells_x,), i...  14.2 us
    ppermute x2, waiting for transfers between devices, fold_halo(): lax.ppermute(lax.slice_in_dim(block, extent - width, None, axis=dim), axi...  10.5 us
    ppermute x2, starting transfers between devices, with_halo(): lax.ppermute(lax.slice_in_dim(block, block.shape[dim] - width, None, axis...  6.1 us
  transfers between devices with their start and end apart: 10, of which 9 were waited for; matrix products, arithmetic and copies ran while one was open for 1% of the time, Pallas kernels for 0%

profile of v1, /device:TPU:0, one launch (start us, length us, event | category | flops | bytes accessed | tf_op | source)
XLA Modules:
  0.0 191.8 jit_solution(12455990615374744632)
XLA Ops:
  0.0 0.9 fusion.1.charge_ref
  0.9 0.0 copy-start
  0.9 0.9 copy-done
  1.9 0.9 copy-done.2
  2.8 14.4 %spread.1 = f32[36,68,256]{2,1,0:T(8,128)S(1)} custom-call(f32[8,16,128]{2,1,0:T(8,128)S(1)} %fusion.1.charge_ref, f32[3,8,16,128]{3,2,1,0:T(8,128)S(1)} %copy-done, s32[3,8,16,128]{3,2,1,0:T(8,128)S(1)} %copy-done.2), custom_call_target="tpu_custom_call" | custom-call | tf_op jit(solution)/shard_map/spread/pallas_call | solution.py:289
  17.2 0.5 collective-permute-start
  17.7 5.7 %collective-permute-done = f32[2,68,256]{2,1,0:T(8,128)S(1)} collective-permute-done((f32[2,68,256]{2,1,0:T(8,128)S(1)}, f32[2,68,256]{2,1,0:T(8,128)S(1)}, u32[]{:S(2)}, u32[]{:S(2)}) %collective-permute-start) | collective-permute-done | bytes 139296 | tf_op jit(solution)/shard_map/ppermute | solution.py:220
  23.5 0.1 collective-permute-start.1
  23.5 0.1 slice.62
  23.7 2.5 %collective-permute-done.1 = f32[2,68,256]{2,1,0:T(8,128)S(1)} collective-permute-done((f32[2,68,256]{2,1,0:T(8,128)S(1)}, f32[2,68,256]{2,1,0:T(8,128)S(1)}, u32[]{:S(2)}, u32[]{:S(2)}) %collective-permute-start.1) | collective-permute-done | bytes 139296 | tf_op jit(solution)/shard_map/ppermute | solution.py:223
  26.3 2.4 %collective-permute-start.2 = (f32[32,2,256]{2,1,0:T(2,128)S(1)}, f32[32,2,256]{2,1,0:T(2,128)S(1)}, u32[]{:S(2)}, u32[]{:S(2)}) collective-permute-start(f32[32,2,256]{2,1,0:T(2,128)S(1)} %pad_maximum_fusion.7), channel_id=1, source_target_pairs={{0,1},{1,2},{2,3},{3,0},{4,5},{5,6},{6,7},{7,4},{8,9},{9,10},{10,1... | collective-permute-start | bytes 196616 | tf_op jit(solution)/shard_map/ppermute | solution.py:220
  28.6 4.8 %collective-permute-done.2 = f32[32,2,256]{2,1,0:T(2,128)S(1)} collective-permute-done((f32[32,2,256]{2,1,0:T(2,128)S(1)}, f32[32,2,256]{2,1,0:T(2,128)S(1)}, u32[]{:S(2)}, u32[]{:S(2)}) %collective-permute-start.2) | collective-permute-done | bytes 65568 | tf_op jit(solution)/shard_map/ppermute | solution.py:220
  33.5 0.1 maximum_add_fusion.1
  33.5 2.1 %collective-permute-start.3 = (f32[32,2,256]{2,1,0:T(2,128)S(1)}, f32[32,2,256]{2,1,0:T(2,128)S(1)}, u32[]{:S(2)}, u32[]{:S(2)}) collective-permute-start(f32[32,2,256]{2,1,0:T(2,128)S(1)} %get-tuple-element.10), channel_id=1, source_target_pairs={{1,0},{2,1},{3,2},{0,3},{5,4},{6,5},{7,6},{4,7},{9,8},{10,9},{11,1... | collective-permute-start | bytes 196616 | tf_op jit(solution)/shard_map/ppermute | solution.py:223
  35.6 0.2 pad_maximum_fusion.1
  35.8 0.3 slice.65
  36.1 1.7 collective-permute-done.3
  37.9 0.0 copy-start.9
  37.9 0.3 pad_maximum_fusion.2.grid_ref
  38.2 0.7 copy-done.9
  38.8 3.2 %depth_forward.1 = f32[4096,128]{1,0:T(8,128)} custom-call(f32[32,64,256]{2,1,0:T(8,128)S(1)} %pad_maximum_fusion.2.grid_ref, bf16[2,256,256]{2,1,0:T(8,128)(2,1)S(1)} %copy-done.9), custom_call_target="tpu_custom_call" | custom-call | tf_op jit(solution)/shard_map/depth_forward/pallas_call | solution.py:301
  42.0 5.3 %all-to-all-start = ((f32[32,128,128]{2,1,0:T(8,128)}), f32[32,128,128]{2,1,0:T(8,128)}, u32[]{:S(2)}, u32[]{:S(2)}) async-start(f32[32,128,128]{2,1,0:T(8,128)} %bitcast.1), calls=%async_computation | async-start | bytes 4194304 | tf_op jit(solution)/shard_map/all_to_all | solution.py:307
  47.4 1.0 slice.55
  48.3 1.3 collective-permute-start.4
  49.6 19.0 %collective-permute-done.4 = f32[1,256,256]{2,1,0:T(8,128)S(1)} collective-permute-done((f32[1,256,256]{2,1,0:T(8,128)S(1)}, f32[1,256,256]{2,1,0:T(8,128)S(1)}, u32[]{:S(2)}, u32[]{:S(2)}) %collective-permute-start.4) | collective-permute-done | bytes 262176 | tf_op jit(solution)/shard_map/ppermute | solution.py:280
  68.6 1.0 dynamic-slice_select_fusion.other_ref
  69.6 25.3 %all-to-all-done = f32[32,128,128]{2,1,0:T(8,128)} async-done(((f32[32,128,128]{2,1,0:T(8,128)}), f32[32,128,128]{2,1,0:T(8,128)}, u32[]{:S(2)}, u32[]{:S(2)}) %all-to-all-start) | async-done | bytes 2097184 | tf_op jit(solution)/shard_map/all_to_all | solution.py:307
  94.9 0.0 copy-done.4
  94.9 0.0 copy-done.5
  94.9 0.0 copy-done.6
  94.9 0.0 copy-done.7
  94.9 14.7 %planes.1 = f32[8,4,8,16,128]{4,3,2,1,0:T(8,128)S(1)} custom-call(s32[1]{0:T(128)} %bitcast.start_ref, f32[8,4,8,16,128]{4,3,2,1,0:T(8,128)} %bitcast.2.in_ref, f32[8,256,256]{2,1,0:T(8,128)} %own_ref.1, f32[1,256,256]{2,1,0:T(8,128)S(1)} %dynamic-slice_select_fusion.other_ref, bf16[2,256,512]{2,1,0:T(8,128)(2,1)S(1)} %copy-done.4, ...), custom_call_target="tpu_custom_call" | custom-call | tf_op jit(solution)/shard_map/planes/pallas_call | solution.py:320
  109.6 0.0 copy-start.8
  109.6 51.5 %all_to_all.20 = f32[32,128,128]{2,1,0:T(8,128)S(1)} all-to-all(f32[32,128,128]{2,1,0:T(8,128)S(1)} %bitcast.5), channel_id=1, replica_groups=mesh['px'=8,'py'=4] {'px','py'}, dimensions={0} | all-to-all | bytes 4194304 | tf_op jit(solution)/shard_map/all_to_all | solution.py:349
  161.1 1.1 depth_inverse.1
  162.2 1.6 collective-permute-start.5
  163.8 1.1 collective-permute-start.6
  165.0 2.6 %collective-permute-done.5 = f32[2,64,256]{2,1,0:T(8,128)S(1)} collective-permute-done((f32[2,64,256]{2,1,0:T(8,128)S(1)}, f32[2,64,256]{2,1,0:T(8,128)S(1)}, u32[]{:S(2)}, u32[]{:S(2)}) %collective-permute-start.5) | collective-permute-done | bytes 131104 | tf_op jit(solution)/shard_map/ppermute | solution.py:206
  167.6 0.0 collective-permute-done.6
  167.6 0.1 pad_maximum_fusion.5
  167.6 4.5 %collective-permute-start.7 = (f32[36,2,256]{2,1,0:T(2,128)S(1)}, f32[36,2,256]{2,1,0:T(2,128)S(1)}, u32[]{:S(2)}, u32[]{:S(2)}) collective-permute-start(f32[36,2,256]{2,1,0:T(2,128)S(1)} %get-tuple-element.7), channel_id=1, source_target_pairs={{0,1},{1,2},{2,3},{3,0},{4,5},{5,6},{6,7},{7,4},{8,9},{9,10},{10,1... | collective-permute-start | bytes 221192 | tf_op jit(solution)/shard_map/ppermute | solution.py:206
  172.1 0.0 collective-permute-start.8
  172.1 2.4 %collective-permute-done.7 = f32[36,2,256]{2,1,0:T(2,128)S(1)} collective-permute-done((f32[36,2,256]{2,1,0:T(2,128)S(1)}, f32[36,2,256]{2,1,0:T(2,128)S(1)}, u32[]{:S(2)}, u32[]{:S(2)}) %collective-permute-start.7) | collective-permute-done | bytes 73760 | tf_op jit(solution)/shard_map/ppermute | solution.py:206
  174.5 2.0 %collective-permute-done.8 = f32[36,2,256]{2,1,0:T(2,128)S(1)} collective-permute-done((f32[36,2,256]{2,1,0:T(2,128)S(1)}, f32[36,2,256]{2,1,0:T(2,128)S(1)}, u32[]{:S(2)}, u32[]{:S(2)}) %collective-permute-start.8) | collective-permute-done | bytes 73760 | tf_op jit(solution)/shard_map/ppermute | solution.py:209
  176.5 0.3 pad_maximum_fusion.grid_ref
  176.8 0.0 copy-start.10
  176.9 14.2 %gather.1 = f32[8,16,128]{2,1,0:T(8,128)S(1)} custom-call(f32[3,8,16,128]{3,2,1,0:T(8,128)S(1)} %copy-done.1, s32[3,8,16,128]{3,2,1,0:T(8,128)S(1)} %copy-done.3, f32[36,68,256]{2,1,0:T(8,128)S(1)} %pad_maximum_fusion.grid_ref), custom_call_target="tpu_custom_call" | custom-call | tf_op jit(solution)/shard_map/gather/pallas_call | solution.py:359
  191.1 0.7 fusion
  (17 shorter events, 0.2 us)
Async XLA Ops:
  0.9 0.9 copy-start
  1.9 0.9 copy-start.2
  17.2 6.2 %collective-permute-start = (f32[2,68,256]{2,1,0:T(8,128)S(1)}, f32[2,68,256]{2,1,0:T(8,128)S(1)}, u32[]{:S(2)}, u32[]{:S(2)}) collective-permute-start(f32[2,68,256]{2,1,0:T(8,128)S(1)} %slice.61), channel_id=1, source_target_pairs={{0,4},{4,8},{8,12},{12,16},{16,20},{20,24},{24,28},{28,0},{1,5},{5... | collective-permute-start | bytes 417800 | tf_op jit(solution)/shard_map/ppermute | solution.py:220
  23.5 2.7 %collective-permute-start.1 = (f32[2,68,256]{2,1,0:T(8,128)S(1)}, f32[2,68,256]{2,1,0:T(8,128)S(1)}, u32[]{:S(2)}, u32[]{:S(2)}) collective-permute-start(f32[2,68,256]{2,1,0:T(8,128)S(1)} %get-tuple-element.6), channel_id=1, source_target_pairs={{4,0},{8,4},{12,8},{16,12},{20,16},{24,20},{28,24},{0,28},{5,1},{9... | collective-permute-start | bytes 417800 | tf_op jit(solution)/shard_map/ppermute | solution.py:223
  26.3 7.2 %collective-permute-start.2 = (f32[32,2,256]{2,1,0:T(2,128)S(1)}, f32[32,2,256]{2,1,0:T(2,128)S(1)}, u32[]{:S(2)}, u32[]{:S(2)}) collective-permute-start(f32[32,2,256]{2,1,0:T(2,128)S(1)} %pad_maximum_fusion.7), channel_id=1, source_target_pairs={{0,1},{1,2},{2,3},{3,0},{4,5},{5,6},{6,7},{7,4},{8,9},{9,10},{10,1... | collective-permute-start | bytes 196616 | tf_op jit(solution)/shard_map/ppermute | solution.py:220
  33.5 4.3 %collective-permute-start.3 = (f32[32,2,256]{2,1,0:T(2,128)S(1)}, f32[32,2,256]{2,1,0:T(2,128)S(1)}, u32[]{:S(2)}, u32[]{:S(2)}) collective-permute-start(f32[32,2,256]{2,1,0:T(2,128)S(1)} %get-tuple-element.10), channel_id=1, source_target_pairs={{1,0},{2,1},{3,2},{0,3},{5,4},{6,5},{7,6},{4,7},{9,8},{10,9},{11,1... | collective-permute-start | bytes 196616 | tf_op jit(solution)/shard_map/ppermute | solution.py:223
  37.9 1.0 copy-start.9
  42.0 52.8 %copy-start.4 = (bf16[2,256,512]{2,1,0:T(8,128)(2,1)S(1)}, bf16[2,256,512]{2,1,0:T(8,128)(2,1)}, u32[]{:S(2)}) copy-start(bf16[2,256,512]{2,1,0:T(8,128)(2,1)} %constant.34.clone.right_ref) | copy-start | bytes 1572868
  42.0 52.8 %copy-start.5 = (bf16[2,256,512]{2,1,0:T(8,128)(2,1)S(1)}, bf16[2,256,512]{2,1,0:T(8,128)(2,1)}, u32[]{:S(2)}) copy-start(bf16[2,256,512]{2,1,0:T(8,128)(2,1)} %constant.35.clone.back_ref) | copy-start | bytes 1572868
  42.0 52.8 %copy-start.6 = (bf16[2,512,256]{2,1,0:T(8,128)(2,1)S(1)}, bf16[2,512,256]{2,1,0:T(8,128)(2,1)}, u32[]{:S(2)}) copy-start(bf16[2,512,256]{2,1,0:T(8,128)(2,1)} %constant.36.clone.left_ref) | copy-start | bytes 1572868
  42.0 52.8 %copy-start.7 = (bf16[2,512,256]{2,1,0:T(8,128)(2,1)S(1)}, bf16[2,512,256]{2,1,0:T(8,128)(2,1)}, u32[]{:S(2)}) copy-start(bf16[2,512,256]{2,1,0:T(8,128)(2,1)} %constant.37.clone.left_back_ref) | copy-start | bytes 1572868
  42.0 52.8 %all-to-all-start = ((f32[32,128,128]{2,1,0:T(8,128)}), f32[32,128,128]{2,1,0:T(8,128)}, u32[]{:S(2)}, u32[]{:S(2)}) async-start(f32[32,128,128]{2,1,0:T(8,128)} %bitcast.1), calls=%async_computation | async-start | bytes 4194304 | tf_op jit(solution)/shard_map/all_to_all | solution.py:307
  48.3 20.3 %collective-permute-start.4 = (f32[1,256,256]{2,1,0:T(8,128)S(1)}, f32[1,256,256]{2,1,0:T(8,128)S(1)}, u32[]{:S(2)}, u32[]{:S(2)}) collective-permute-start(f32[1,256,256]{2,1,0:T(8,128)S(1)} %slice.55), channel_id=1, source_target_pairs={{16,0}} | collective-permute-start | bytes 786440 | tf_op jit(solution)/shard_map/ppermute | solution.py:280
  109.6 51.5 %copy-start.8 = (bf16[2,256,256]{2,1,0:T(8,128)(2,1)S(1)}, bf16[2,256,256]{2,1,0:T(8,128)(2,1)}, u32[]{:S(2)}) copy-start(bf16[2,256,256]{2,1,0:T(8,128)(2,1)} %constant.38.clone.table_ref) | copy-start | bytes 786436
  162.2 5.3 %collective-permute-start.5 = (f32[2,64,256]{2,1,0:T(8,128)S(1)}, f32[2,64,256]{2,1,0:T(8,128)S(1)}, u32[]{:S(2)}, u32[]{:S(2)}) collective-permute-start(f32[2,64,256]{2,1,0:T(8,128)S(1)} %get-tuple-element.11), channel_id=1, source_target_pairs={{0,4},{4,8},{8,12},{12,16},{16,20},{20,24},{24,28},{28,0},{1,5},{5... | collective-permute-start | bytes 393224 | tf_op jit(solution)/shard_map/ppermute | solution.py:206
  163.8 3.7 %collective-permute-start.6 = (f32[2,64,256]{2,1,0:T(8,128)S(1)}, f32[2,64,256]{2,1,0:T(8,128)S(1)}, u32[]{:S(2)}, u32[]{:S(2)}) collective-permute-start(f32[2,64,256]{2,1,0:T(8,128)S(1)} %get-tuple-element.12), channel_id=1, source_target_pairs={{4,0},{8,4},{12,8},{16,12},{20,16},{24,20},{28,24},{0,28},{5,1},{9... | collective-permute-start | bytes 393224 | tf_op jit(solution)/shard_map/ppermute | solution.py:209
  167.6 6.9 %collective-permute-start.7 = (f32[36,2,256]{2,1,0:T(2,128)S(1)}, f32[36,2,256]{2,1,0:T(2,128)S(1)}, u32[]{:S(2)}, u32[]{:S(2)}) collective-permute-start(f32[36,2,256]{2,1,0:T(2,128)S(1)} %get-tuple-element.7), channel_id=1, source_target_pairs={{0,1},{1,2},{2,3},{3,0},{4,5},{5,6},{6,7},{7,4},{8,9},{9,10},{10,1... | collective-permute-start | bytes 221192 | tf_op jit(solution)/shard_map/ppermute | solution.py:206
  172.1 4.7 %copy-start.1 = (f32[3,8,16,128]{3,2,1,0:T(8,128)S(1)}, f32[3,8,16,128]{3,2,1,0:T(8,128)}, u32[]{:S(2)}) copy-start(f32[3,8,16,128]{3,2,1,0:T(8,128)} %fraction_ref.3) | copy-start | bytes 589828
  172.1 4.7 %copy-start.3 = (s32[3,8,16,128]{3,2,1,0:T(8,128)S(1)}, s32[3,8,16,128]{3,2,1,0:T(8,128)}, u32[]{:S(2)}) copy-start(s32[3,8,16,128]{3,2,1,0:T(8,128)} %base_ref.3) | copy-start | bytes 589828
  172.1 4.4 %collective-permute-start.8 = (f32[36,2,256]{2,1,0:T(2,128)S(1)}, f32[36,2,256]{2,1,0:T(2,128)S(1)}, u32[]{:S(2)}, u32[]{:S(2)}) collective-permute-start(f32[36,2,256]{2,1,0:T(2,128)S(1)} %get-tuple-element.8), channel_id=1, source_target_pairs={{1,0},{2,1},{3,2},{0,3},{5,4},{6,5},{7,6},{4,7},{9,8},{10,9},{11,1... | collective-permute-start | bytes 221192 | tf_op jit(solution)/shard_map/ppermute | solution.py:209
  176.8 14.2 %copy-start.10 = (s32[8,16]{1,0:T(8,128)S(1)}, s32[8,16]{1,0:T(8,128)}, u32[]{:S(2)}) copy-start(s32[8,16]{1,0:T(8,128)} %param.14) | copy-start | bytes 1540

commit v2 on v1

--- a/solution.py
+++ b/solution.py
@@ -13,6 +13,7 @@
 CELL = 4
 REACH = 8
 VMEM_LIMIT = 48 * 1024 * 1024
+MESH = pl.DeviceIdType.MESH
 
 
 def halves_np(table):
@@ -134,23 +135,113 @@
         )
 
 
-def plane_kernel(
-    start_ref, in_ref, own_ref, other_ref, right_ref, back_ref, left_ref, left_back_ref, out_ref
+def exchange_kernel(
+    count_x,
+    count_y,
+    send_ref,
+    influence_ref,
+    right_ref,
+    back_ref,
+    left_ref,
+    left_back_ref,
+    out_ref,
+    taken,
+    turned,
+    other,
+    taken_sent,
+    taken_here,
+    turned_sent,
+    turned_here,
+    plane_sent,
+    plane_here,
 ):
-    count_x, count_y, parts, pairs, lanes = in_ref.shape
+    devices, planes, parts, pairs, lanes = send_ref.shape
     half = lanes // 2
     rows = count_x * pairs
     full_y = count_y * half
     full_x = 2 * rows
+    my_x, my_y = lax.axis_index("px"), lax.axis_index("py")
+    me = my_x * count_y + my_y
+    start = jnp.where(me < devices // 2, 0, 1)
+
+    def peer(step):
+        index = lax.rem(me + step, devices)
+        return index, (index // count_y, lax.rem(index, count_y))
+
+    barrier = pltpu.get_barrier_semaphore()
+
+    @pl.loop(1, devices)
+    def _(step):
+        pl.semaphore_signal(barrier, inc=1, device_id=peer(step)[1], device_id_type=MESH)
+
+    pl.semaphore_wait(barrier, devices - 1)
+
+    lone = pltpu.make_async_remote_copy(
+        src_ref=influence_ref.at[0],
+        dst_ref=other,
+        send_sem=plane_sent,
+        recv_sem=plane_here,
+        device_id=(0, 0),
+        device_id_type=MESH,
+    )
+
+    @pl.when(me == devices // 2)
+    def _():
+        lone.start()
+
+    @pl.loop(0, planes)
+    def _(plane):
+        @pl.loop(1, devices)
+        def _(step):
+            index, place = peer(step)
+            pltpu.make_async_remote_copy(
+                src_ref=send_ref.at[index, plane],
+                dst_ref=taken.at[plane, me],
+                send_sem=taken_sent.at[plane],
+                recv_sem=taken_here.at[plane],
+                device_id=place,
+                device_id_type=MESH,
+            ).start()
+
+        taken[plane, me] = send_ref[me, plane]
+
+    @pl.when(me == devices // 2)
+    def _():
+        lone.wait_send()
+
+    @pl.when(me == 0)
+    def _():
+        lone.wait_recv()
+
+    @pl.when(me != 0)
+    def _():
+        other[...] = influence_ref[start]
+
+    def others(buffer, plane, sent, here):
+        chunk = buffer.at[plane, pl.ds(0, devices - 1)]
+        return pltpu.make_async_remote_copy(
+            src_ref=chunk,
+            dst_ref=chunk,
+            send_sem=sent.at[plane],
+            recv_sem=here.at[plane],
+            device_id=peer(1)[1],
+            device_id_type=MESH,
+        )
+
     right = (right_ref[0], right_ref[1])
     back = (back_ref[0], back_ref[1])
     left = (left_ref[0], left_ref[1])
     left_back = (left_back_ref[0], left_back_ref[1])
 
-    def load(part):
-        blocks = [in_ref[:, y, part].reshape(rows, lanes) for y in range(count_y)]
-        top = jnp.concatenate([block[:, :half] for block in blocks], axis=1)
-        bottom = jnp.concatenate([block[:, half:] for block in blocks], axis=1)
+    def load(plane, part):
+        columns = [
+            jnp.concatenate(
+                [taken[plane, x * count_y + y, part] for x in range(count_x)], axis=0
+            )
+            for y in range(count_y)
+        ]
+        top = jnp.concatenate([block[:, :half] for block in columns], axis=1)
+        bottom = jnp.concatenate([block[:, half:] for block in columns], axis=1)
         return jnp.concatenate([top, bottom], axis=0)
 
     def along_x(table, real, imag):
@@ -161,13 +252,16 @@
             upper[:, full_y:] + lower[:, :full_y],
         )
 
-    first = dot3(halves(load(0)), right, NN)
-    second = dot3(halves(load(1)), right, NN)
-    first = (first[:, :full_y], first[:, full_y:])
-    second = (second[:, :full_y], second[:, full_y:])
-
-    def finish(real, imag):
-        real, imag = along_x(left_back, real, imag)
+    @pl.loop(0, planes)
+    def _(plane):
+        others(taken, plane, taken_sent, taken_here).wait_recv()
+        first = dot3(halves(load(plane, 0)), right, NN)
+        second = dot3(halves(load(plane, 1)), right, NN)
+        ar, ai = along_x(left, first[:, :full_y], first[:, full_y:])
+        br, bi = along_x(left, second[:, :full_y], second[:, full_y:])
+        own = influence_ref[start + plane]
+        mate = jnp.where(plane == 0, other[...], own)
+        real, imag = along_x(left_back, own * ar - mate * bi, own * ai + mate * br)
         both = dot3(halves(jnp.concatenate([real, imag], axis=0)), back, NN)
         upper, lower = both[:full_x], both[full_x:]
         results = (
@@ -180,60 +274,130 @@
                 columns = slice(y * half, (y + 1) * half)
                 block = jnp.concatenate(
                     [result[:rows, columns], result[rows:, columns]], axis=1
+                ).reshape(count_x, pairs, lanes)
+                for x in range(count_x):
+                    turned[plane, x * count_y + y, part] = block[x]
+
+        @pl.loop(1, devices)
+        def _(step):
+            index, place = peer(step)
+            pltpu.make_async_remote_copy(
+                src_ref=turned.at[plane, index],
+                dst_ref=out_ref.at[me, plane],
+                send_sem=turned_sent.at[plane],
+                recv_sem=turned_here.at[plane],
+                device_id=place,
+                device_id_type=MESH,
+            ).start()
+
+        out_ref[me, plane] = turned[plane, me]
+
+    @pl.loop(0, planes)
+    def _(plane):
+        others(taken, plane, taken_sent, taken_here).wait_send()
+        last = others(turned, plane, turned_sent, turned_here)
+        last.wait_send()
+        last.wait_recv()
+
+
+def neighbour_copies(count_x, count_y, row_out, row_in, col_out, col_in, edge_out, edge_in, sent, here):
+    my_x, my_y = lax.axis_index("px"), lax.axis_index("py")
+
+    def place(dx, dy):
+        return lax.rem(my_x + dx + count_x, count_x), lax.rem(my_y + dy + count_y, count_y)
+
+    shifts = (-1, 1)
+    plan = [(row_out.at[i], row_in.at[i], place(shifts[i], 0)) for i in range(2)]
+    plan += [(col_out.at[i], col_in.at[i], place(0, shifts[i])) for i in range(2)]
+    plan += [
+        (edge_out.at[2 * i + j], edge_in.at[2 * i + j], place(shifts[i], shifts[j]))
+        for i in range(2)
+        for j in range(2)
+    ]
+    barrier = pltpu.get_barrier_semaphore()
+    for _, _, device in plan:
+        pl.semaphore_signal(barrier, inc=1, device_id=device, device_id_type=MESH)
+    pl.semaphore_wait(barrier, len(plan))
+    copies = [
+        pltpu.make_async_remote_copy(
+            src_ref=source,
+            dst_ref=target,
+            send_sem=sent.at[k],
+            recv_sem=here.at[k],
+            device_id=device,
+            device_id_type=MESH,
+        )
+        for k, (source, target, device) in enumerate(plan)
+    ]
+    return copies
+
+
+def fold_kernel(count_x, count_y, in_ref, out_ref, *scratch):
+    row_out, row_in, col_out, col_in, edge_out, edge_in, sent, here = scratch
+    nx, ny, size = out_ref.shape
+    for i in range(2):
+        x = (0, nx + 2)[i]
+        y = (0, ny + 2)[i]
+        row_out[i] = in_ref[x : x + 2, 2 : ny + 2, :]
+        for j in range(2):
+            col_out[i, j] = in_ref[2 : nx + 2, y + j, :]
+            edge = (0, ny + 2)[j]
+            for k in range(2):
+                edge_out[2 * i + j, 2 * k : 2 * k + 2] = in_ref[x + k, edge : edge + 2, :]
+    copies = neighbour_copies(count_x, count_y, *scratch)
+    for copy in copies:
+        copy.start()
+    out_ref[...] = in_ref[2 : nx + 2, 2 : ny + 2, :]
+    for copy in copies:
+        copy.wait()
+    for i in range(2):
+        x = (nx - 2, 0)[i]
+        y = (ny - 2, 0)[i]
+        out_ref[x : x + 2] = out_ref[x : x + 2] + row_in[i]
+        for j in range(2):
+            out_ref[:, y + j, :] = out_ref[:, y + j, :] + col_in[i, j]
+            edge = (ny - 2, 0)[j]
+            for k in range(2):
+                out_ref[x + k, edge : edge + 2, :] = (
+                    out_ref[x + k, edge : edge + 2, :] + edge_in[2 * i + j, 2 * k : 2 * k + 2]
                 )
-                out_ref[:, y, part] = block.reshape(count_x, pairs, lanes)
-
-    own = own_ref[0]
-
-    @pl.when(pl.program_id(0) == 0)
-    def _():
-        other = other_ref[0]
-        ar, ai = along_x(left, *first)
-        br, bi = along_x(left, *second)
-        finish(own * ar - other * bi, own * ai + other * br)
-
-    @pl.when(pl.program_id(0) != 0)
-    def _():
-        real, imag = along_x(left, first[0] - second[1], first[1] + second[0])
-        finish(own * real, own * imag)
-
-
-def with_halo(block, sides, width):
-    for axis, dim in sides:
-        count = lax.axis_size(axis)
-        forward = [(i, (i + 1) % count) for i in range(count)]
-        backward = [(target, source) for source, target in forward]
-        low = lax.ppermute(
-            lax.slice_in_dim(block, block.shape[dim] - width, None, axis=dim), axis, forward
-        )
-        high = lax.ppermute(lax.slice_in_dim(block, 0, width, axis=dim), axis, backward)
-        block = jnp.concatenate([low, block, high], axis=dim)
-    return block
-
-
-def fold_halo(block, sides, width):
-    for axis, dim in sides:
-        count = lax.axis_size(axis)
-        extent = block.shape[dim]
-        forward = [(i, (i + 1) % count) for i in range(count)]
-        backward = [(target, source) for source, target in forward]
-        low = lax.ppermute(
-            lax.slice_in_dim(block, extent - width, None, axis=dim), axis, forward
-        )
-        high = lax.ppermute(lax.slice_in_dim(block, 0, width, axis=dim), axis, backward)
-
-        def part(start, stop):
-            return lax.slice_in_dim(block, start, stop, axis=dim)
-
-        block = jnp.concatenate(
-            [
-                part(width, 2 * width) + low,
-                part(2 * width, extent - 2 * width),
-                part(extent - 2 * width, extent - width) + high,
-            ],
-            axis=dim,
-        )
-    return block
+
+
+def halo_kernel(count_x, count_y, in_ref, out_ref, *scratch):
+    row_out, row_in, col_out, col_in, edge_out, edge_in, sent, here = scratch
+    nx, ny, size = in_ref.shape
+    for i in range(2):
+        x = (0, nx - 2)[i]
+        y = (0, ny - 2)[i]
+        row_out[i] = in_ref[x : x + 2]
+        for j in range(2):
+            col_out[i, j] = in_ref[:, y + j, :]
+            edge = (0, ny - 2)[j]
+            for k in range(2):
+                edge_out[2 * i + j, 2 * k : 2 * k + 2] = in_ref[x + k, edge : edge + 2, :]
+    copies = neighbour_copies(count_x, count_y, *scratch)
+    for copy in copies:
+        copy.start()
+    out_ref[2 : nx + 2, 2 : ny + 2, :] = in_ref[...]
+    for copy in copies:
+        copy.wait()
+    for i in range(2):
+        x = (nx + 2, 0)[i]
+        y = (ny + 2, 0)[i]
+        out_ref[x : x + 2, 2 : ny + 2, :] = row_in[i]
+        for j in range(2):
+            out_ref[2 : nx + 2, y + j, :] = col_in[i, j]
+            edge = (ny + 2, 0)[j]
+            for k in range(2):
+                out_ref[x + k, edge : edge + 2, :] = edge_in[2 * i + j, 2 * k : 2 * k + 2]
+
+
+def halo_scratch(nx, ny, size):
+    shapes = [(2, 2, ny, size)] * 2 + [(2, 2, nx, size)] * 2 + [(4, 4, size)] * 2
+    return [pltpu.VMEM(shape, jnp.float32) for shape in shapes] + [
+        pltpu.SemaphoreType.DMA((8,)),
+        pltpu.SemaphoreType.DMA((8,)),
+    ]
 
 
 def wave_tables(size, devices, scale):
@@ -272,15 +436,13 @@
     pairs = local_x // 2
     lanes = 2 * local_y
     params = pltpu.CompilerParams(vmem_limit_bytes=VMEM_LIMIT)
-    device = lax.axis_index("px") * py_size + lax.axis_index("py")
-
     occupied = jnp.arange(slots, dtype=jnp.int32)[None, None, :] < cell_count[:, :, None]
     charge = jnp.where(occupied, cotangent, 0.0)
 
-    extra = lax.ppermute(influence[:1], ("px", "py"), [(devices // 2, 0)])
-    start = jnp.where(device < devices // 2, 0, 1).astype(jnp.int32)
-    own_first = lax.dynamic_slice_in_dim(influence, start, 1, axis=0)
-    other = jnp.where(device == 0, extra, own_first)
+    def linked(number):
+        return pltpu.CompilerParams(
+            vmem_limit_bytes=VMEM_LIMIT, collective_id=number, has_side_effects=True
+        )
 
     whole = lambda *dims: pl.BlockSpec(dims, lambda *_: (0,) * len(dims))
     atoms = pl.BlockSpec((3, 1, cells_y, slots), lambda i: (0, i, 0, 0))
@@ -295,7 +457,13 @@
         compiler_params=params,
         name="spread",
     )(charge, fraction, grid_base)
-    spread = fold_halo(extended, (("px", 0), ("py", 1)), 2)
+    spread = pl.pallas_call(
+        functools.partial(fold_kernel, px_size, py_size),
+        out_shape=jax.ShapeDtypeStruct((local_x, local_y, size), jnp.float32),
+        scratch_shapes=halo_scratch(local_x, local_y, size),
+        compiler_params=linked(0),
+        name="fold",
+    )(extended)
 
     forward_z, inverse_z = wave_tables(size, devices, 1.0 / (size * full_x * full_y))
     columns = pl.pallas_call(
@@ -304,9 +472,6 @@
         compiler_params=params,
         name="depth_forward",
     )(spread, halves_np(forward_z))
-    mixed = lax.all_to_all(columns, ("px", "py"), split_axis=0, concat_axis=0, tiled=True)
-    mixed = mixed.reshape(px_size, py_size, 2 * planes, pairs, lanes)
-
     order = np.arange(full_x).reshape(full_x // 2, 2).T.reshape(-1)
     y_angles = angles(np.arange(full_y), np.arange(full_y), full_y)
     x_angles = angles(np.arange(full_x), order, full_x)
@@ -314,48 +479,40 @@
     back = np.concatenate([np.cos(y_angles), np.sin(y_angles)], axis=1)
     left = np.concatenate([np.cos(x_angles), -np.sin(x_angles)], axis=0)
     left_back = np.concatenate([np.cos(x_angles.T), np.sin(x_angles.T)], axis=0)
-    block = pl.BlockSpec(
-        (px_size, py_size, 2, pairs, lanes), lambda i, start: (0, 0, i, 0, 0)
-    )
-    turned = pl.pallas_call(
-        plane_kernel,
-        grid_spec=pltpu.PrefetchScalarGridSpec(
-            num_scalar_prefetch=1,
-            grid=(planes,),
-            in_specs=[
-                block,
-                pl.BlockSpec((1, full_x, full_y), lambda i, start: (i + start[0], 0, 0)),
-                whole(1, full_x, full_y),
-                whole(2, full_y, 2 * full_y),
-                whole(2, full_y, 2 * full_y),
-                whole(2, 2 * full_x, full_x),
-                whole(2, 2 * full_x, full_x),
-            ],
-            out_specs=block,
-        ),
-        out_shape=jax.ShapeDtypeStruct(mixed.shape, jnp.float32),
-        compiler_params=params,
-        name="planes",
+    chunks = (devices, planes, 2, pairs, lanes)
+    landing = pltpu.VMEM((planes, devices, 2, pairs, lanes), jnp.float32)
+    in_vmem = pl.BlockSpec(memory_space=pltpu.VMEM)
+    returned = pl.pallas_call(
+        functools.partial(exchange_kernel, px_size, py_size),
+        in_specs=[in_vmem] * 6,
+        out_specs=in_vmem,
+        out_shape=jax.ShapeDtypeStruct(chunks, jnp.float32),
+        scratch_shapes=[landing, landing, pltpu.VMEM((full_x, full_y), jnp.float32)]
+        + [pltpu.SemaphoreType.DMA((planes,))] * 4
+        + [pltpu.SemaphoreType.DMA] * 2,
+        compiler_params=linked(1),
+        name="exchange",
     )(
-        start[None],
-        mixed,
+        columns.reshape(chunks),
         influence,
-        other,
         halves_np(right),
         halves_np(back),
         halves_np(left),
         halves_np(left_back),
-    )
-    returned = lax.all_to_all(
-        turned.reshape(size * pairs, lanes), ("px", "py"), split_axis=0, concat_axis=0, tiled=True
-    )
+    ).reshape(size * pairs, lanes)
     potential = pl.pallas_call(
         depth_inverse_kernel,
         out_shape=jax.ShapeDtypeStruct((local_x, local_y, size), jnp.float32),
         compiler_params=params,
         name="depth_inverse",
     )(returned, halves_np(inverse_z))
-    halo_potential = with_halo(potential, (("px", 0), ("py", 1)), 2)
+    halo_potential = pl.pallas_call(
+        functools.partial(halo_kernel, px_size, py_size),
+        out_shape=jax.ShapeDtypeStruct(extended.shape, jnp.float32),
+        scratch_shapes=halo_scratch(local_x, local_y, size),
+        compiler_params=linked(2),
+        name="halo",
+    )(potential)
     gradient = pl.pallas_call(
         functools.partial(gather_kernel, size),
         grid=(cells_x,),

time: 192 us -> 156 us (0.81)
  Pallas kernels: 47.6 us -> 151 us
  waiting for transfers between devices: 66 us -> 0 us
  blocking collectives: 51.5 us -> 0 us
  starting transfers between devices: 18.9 us -> 0 us
  other arithmetic: 3.59 us -> 1.64 us
    pallas_call x1 -> x3, Pallas kernels: 14.7 us -> 119 us  [the longest x1 98.3 us: per_device(): pl.pallas_call(functools.partial(exchange_kernel, px_size, py_size), in_s...]
    all_to_all x1 -> x0, blocking collectives: 51.5 us -> none  [per_device(): lax.all_to_all(turned.reshape(size * pairs, lanes), ('px', 'py'), split_a...]
    ppermute x9 -> x0, waiting for transfers between devices: 40.7 us -> none  [the longest x1 19 us: per_device(): extra = lax.ppermute(influence[:1], ('px', 'py'), [(devices // 2, 0)])]
    all_to_all x1 -> x0, waiting for transfers between devices: 25.3 us -> none  [per_device(): lax.all_to_all(columns, ('px', 'py'), split_axis=0, concat_axis=0, tiled=...]
    ppermute x9 -> x0, starting transfers between devices: 13.6 us -> none  [the longest x2 6.1 us: with_halo(): lax.ppermute(lax.slice_in_dim(block, block.shape[dim] - width, None, axis...]
    all_to_all x1 -> x0, starting transfers between devices: 5.32 us -> none  [per_device(): lax.all_to_all(columns, ('px', 'py'), split_axis=0, concat_axis=0, tiled=...]
  transfers between devices with their start and end apart: 10 -> 0, of which waited for: 9 -> 0; matrix products, arithmetic and copies ran while one was open for 1% -> 0% of each run, Pallas kernels for 0% -> 0%
where the time goes in v2:
time: 156 us
  Pallas kernels  151 us (97%)
  local copies, waits for them, and re-layouts  3.23 us (2%)
  other arithmetic  1.64 us (1%)
    pallas_call x1, Pallas kernels, per_device(): pl.pallas_call(functools.partial(exchange_kernel, px_size, py_size), in_s...  98.3 us
    pallas_call x1, Pallas kernels, per_device(): pl.pallas_call(functools.partial(spread_kernel, size), grid=(cells_x,), i...  14.4 us
    pallas_call x1, Pallas kernels, per_device(): pl.pallas_call(functools.partial(gather_kernel, size), grid=(cells_x,), i...  14.2 us
    pallas_call x1, Pallas kernels, per_device(): pl.pallas_call(functools.partial(fold_kernel, px_size, py_size), out_shap...  11.5 us
    pallas_call x1, Pallas kernels, per_device(): pl.pallas_call(functools.partial(halo_kernel, px_size, py_size), out_shap...  9.44 us
    unnamed x24, local copies, waits for them, and re-layouts  3.23 us

profile of v2, /device:TPU:0, one launch (start us, length us, event | category | flops | bytes accessed | tf_op | source)
XLA Modules:
  0.0 155.9 jit_solution(7651671920271567705)
XLA Ops:
  0.0 0.9 fusion.1.charge_ref
  0.9 0.0 copy-start.1
  0.9 0.9 copy-done.1
  1.9 0.0 copy-start.3
  1.9 0.9 copy-done.3
  2.8 14.4 %spread.1.in_ref = f32[36,68,256]{2,1,0:T(8,128)S(1)} custom-call(f32[8,16,128]{2,1,0:T(8,128)S(1)} %fusion.1.charge_ref, f32[3,8,16,128]{3,2,1,0:T(8,128)S(1)} %copy-done.1, s32[3,8,16,128]{3,2,1,0:T(8,128)S(1)} %copy-done.3), custom_call_target="tpu_custom_call" | custom-call | tf_op jit(solution)/shard_map/spread/pallas_call | solution.py:451
  17.2 0.0 copy-start.9
  17.2 11.5 %fold.1.grid_ref = f32[32,64,256]{2,1,0:T(8,128)S(1)} custom-call(f32[36,68,256]{2,1,0:T(8,128)S(1)} %spread.1.in_ref), custom_call_target="tpu_custom_call" | custom-call | tf_op jit(solution)/shard_map/fold/pallas_call | solution.py:460
  28.7 0.0 copy-done.9
  28.7 0.0 copy-start.5
  28.7 0.0 copy-start.6
  28.7 0.0 copy-start.7
  28.8 0.0 copy-start.8
  28.8 1.9 %depth_forward.1 = f32[4096,128]{1,0:T(8,128)S(1)} custom-call(f32[32,64,256]{2,1,0:T(8,128)S(1)} %fold.1.grid_ref, bf16[2,256,256]{2,1,0:T(8,128)(2,1)S(1)} %copy-done.9), custom_call_target="tpu_custom_call" | custom-call | tf_op jit(solution)/shard_map/depth_forward/pallas_call | solution.py:469
  30.7 0.0 copy-start
  30.7 1.3 copy-done
  32.0 0.0 copy-done.5
  32.0 0.0 copy-done.6
  32.0 0.0 copy-done.7
  32.0 0.0 copy-done.8
  32.0 0.0 copy-start.10
  32.0 98.3 %exchange.1 = f32[32,4,2,16,128]{4,3,2,1,0:T(8,128)S(1)} custom-call(f32[32,4,2,16,128]{4,3,2,1,0:T(8,128)} %bitcast.2, f32[8,256,256]{2,1,0:T(8,128)} %influence_ref.1, bf16[2,256,512]{2,1,0:T(8,128)(2,1)S(1)} %copy-done.8, bf16[2,256,512]{2,1,0:T(8,128)(2,1)S(1)} %copy-done.7, bf16[2,512,256]{2,1,0:T(8,128)(2,1)S(1)} %copy-done.6, ...), custom_call_target="tpu_custom_call" | custom-call | tf_op jit(solution)/shard_map/exchange/pallas_call | solution.py:485
  130.3 0.0 copy-done.10
  130.3 1.1 depth_inverse.1.in_ref
  131.5 0.0 copy-start.2
  131.5 0.0 copy-start.4
  131.5 9.4 %halo.1.grid_ref = f32[36,68,256]{2,1,0:T(8,128)S(1)} custom-call(f32[32,64,256]{2,1,0:T(8,128)S(1)} %depth_inverse.1.in_ref), custom_call_target="tpu_custom_call" | custom-call | tf_op jit(solution)/shard_map/halo/pallas_call | solution.py:509
  140.9 0.0 copy-done.2
  140.9 0.0 copy-done.4
  141.0 0.0 copy-start.11
  141.0 14.2 %gather.1 = f32[8,16,128]{2,1,0:T(8,128)S(1)} custom-call(f32[3,8,16,128]{3,2,1,0:T(8,128)S(1)} %copy-done.2, s32[3,8,16,128]{3,2,1,0:T(8,128)S(1)} %copy-done.4, f32[36,68,256]{2,1,0:T(8,128)S(1)} %halo.1.grid_ref), custom_call_target="tpu_custom_call" | custom-call | tf_op jit(solution)/shard_map/gather/pallas_call | solution.py:516
  155.2 0.0 copy-done.11
  155.2 0.7 fusion
Async XLA Ops:
  0.9 0.9 copy-start.1
  1.9 0.9 copy-start.3
  17.2 11.5 %copy-start.9 = (bf16[2,256,256]{2,1,0:T(8,128)(2,1)S(1)}, bf16[2,256,256]{2,1,0:T(8,128)(2,1)}, u32[]{:S(2)}) copy-start(bf16[2,256,256]{2,1,0:T(8,128)(2,1)} %constant.14.clone.table_ref) | copy-start | bytes 786436
  28.7 3.3 %copy-start.5 = (bf16[2,512,256]{2,1,0:T(8,128)(2,1)S(1)}, bf16[2,512,256]{2,1,0:T(8,128)(2,1)}, u32[]{:S(2)}) copy-start(bf16[2,512,256]{2,1,0:T(8,128)(2,1)} %constant.18.clone.left_back_ref) | copy-start | bytes 1572868
  28.7 3.3 %copy-start.6 = (bf16[2,512,256]{2,1,0:T(8,128)(2,1)S(1)}, bf16[2,512,256]{2,1,0:T(8,128)(2,1)}, u32[]{:S(2)}) copy-start(bf16[2,512,256]{2,1,0:T(8,128)(2,1)} %constant.17.clone.left_ref) | copy-start | bytes 1572868
  28.7 3.3 %copy-start.7 = (bf16[2,256,512]{2,1,0:T(8,128)(2,1)S(1)}, bf16[2,256,512]{2,1,0:T(8,128)(2,1)}, u32[]{:S(2)}) copy-start(bf16[2,256,512]{2,1,0:T(8,128)(2,1)} %constant.16.clone.back_ref) | copy-start | bytes 1572868
  28.8 3.2 %copy-start.8 = (bf16[2,256,512]{2,1,0:T(8,128)(2,1)S(1)}, bf16[2,256,512]{2,1,0:T(8,128)(2,1)}, u32[]{:S(2)}) copy-start(bf16[2,256,512]{2,1,0:T(8,128)(2,1)} %constant.15.clone.right_ref) | copy-start | bytes 1572868
  30.7 1.3 copy-start
  32.0 98.3 %copy-start.10 = (bf16[2,256,256]{2,1,0:T(8,128)(2,1)S(1)}, bf16[2,256,256]{2,1,0:T(8,128)(2,1)}, u32[]{:S(2)}) copy-start(bf16[2,256,256]{2,1,0:T(8,128)(2,1)} %constant.19.clone.table_ref) | copy-start | bytes 786436
  131.5 9.5 %copy-start.2 = (f32[3,8,16,128]{3,2,1,0:T(8,128)S(1)}, f32[3,8,16,128]{3,2,1,0:T(8,128)}, u32[]{:S(2)}) copy-start(f32[3,8,16,128]{3,2,1,0:T(8,128)} %fraction_ref.3) | copy-start | bytes 589828
  131.5 9.5 %copy-start.4 = (s32[3,8,16,128]{3,2,1,0:T(8,128)S(1)}, s32[3,8,16,128]{3,2,1,0:T(8,128)}, u32[]{:S(2)}) copy-start(s32[3,8,16,128]{3,2,1,0:T(8,128)} %base_ref.3) | copy-start | bytes 589828
  141.0 14.2 %copy-start.11 = (s32[8,16]{1,0:T(8,128)S(1)}, s32[8,16]{1,0:T(8,128)}, u32[]{:S(2)}) copy-start(s32[8,16]{1,0:T(8,128)} %param.14) | copy-start | bytes 1540

commit v3 on v2

--- a/solution.py
+++ b/solution.py
@@ -65,54 +65,48 @@
 
 
 def depth_weights(base, weights, size):
-    level = lax.broadcasted_iota(jnp.int32, (size, base.shape[1]), 0)
-    selected = (base + 2 - level) & (size - 1)
-    total = jnp.zeros(selected.shape, jnp.float32)
+    slots = base.shape[1]
+    tile, shape = (16, slots), (size // 16, 16, slots)
+    inner = lax.broadcasted_iota(jnp.int32, tile, 0)
+    anchor = (jnp.broadcast_to(base + 2, tile) - inner).astype(jnp.int16)[None]
+    level = (16 * lax.broadcasted_iota(jnp.int32, shape, 0)).astype(jnp.int16)
+    selected = (anchor - level) & jnp.int16(size - 1)
+    high = jnp.zeros(shape, jnp.bfloat16)
+    low = jnp.zeros(shape, jnp.bfloat16)
     for degree in range(5):
-        total = jnp.where(selected == degree, weights[degree], total)
-    return total
-
-
-def cell_tables(across, base_ref, cell, size):
+        here = selected == jnp.int16(degree)
+        upper, lower = halves(jnp.broadcast_to(weights[degree], tile))
+        high = jnp.where(here, upper[None], high)
+        low = jnp.where(here, lower[None], low)
+    return high.reshape(size, slots), low.reshape(size, slots)
+
+
+def cell_tables(across, base_ref, index, cell, size):
     def row(values):
         return [value[cell : cell + 1, :] for value in values]
 
-    window_x = window_weights(base_ref[0, 0, cell : cell + 1, :] & (CELL - 1), row(across[0]))
-    window_y = window_weights(base_ref[1, 0, cell : cell + 1, :] & (CELL - 1), row(across[1]))
-    depth = depth_weights(base_ref[2, 0, cell : cell + 1, :], row(across[2]), size)
-    return window_x, window_y, halves(depth)
-
-
-def spread_kernel(size, charge_ref, fraction_ref, base_ref, out_ref):
-    row = pl.program_id(0)
-
-    @pl.when(row == 0)
-    def _():
-        out_ref[...] = jnp.zeros_like(out_ref)
-
-    across = [spline_weights(fraction_ref[dim, 0]) for dim in range(3)]
-    charge = charge_ref[0]
-    cells_y, slots = charge.shape
-    for cell in range(cells_y):
-        window_x, window_y, depth = cell_tables(across, base_ref, cell, size)
-        loaded = charge[cell : cell + 1, :] * window_x
-        lifted = (loaded[:, None, :] * window_y[None, :, :]).reshape(REACH * REACH, slots)
-        patch = dot3(halves(lifted), depth, NT).reshape(REACH, REACH, size)
-        span = (pl.ds(row * CELL, REACH), pl.ds(cell * CELL, REACH), slice(None))
-        out_ref[span] = out_ref[span] + patch
-
-
-def gather_kernel(size, fraction_ref, base_ref, grid_ref, out_ref):
-    row = pl.program_id(0)
-    across = [spline_weights(fraction_ref[dim, 0]) for dim in range(3)]
-    cells_y, slots = fraction_ref.shape[2:]
-    for cell in range(cells_y):
-        window_x, window_y, depth = cell_tables(across, base_ref, cell, size)
-        span = (pl.ds(row * CELL, REACH), pl.ds(cell * CELL, REACH), slice(None))
-        window = grid_ref[span].reshape(REACH * REACH, size)
-        value = dot3(halves(window), depth, NN).reshape(REACH, REACH, slots)
-        value = jnp.sum(value * window_x[:, None, :], axis=0) * window_y
-        out_ref[0, cell : cell + 1, :] = jnp.sum(value, axis=0, keepdims=True)
+    def base(dim):
+        return base_ref[dim, index, cell : cell + 1, :]
+
+    window_x = window_weights(base(0) & (CELL - 1), row(across[0]))
+    window_y = window_weights(base(1) & (CELL - 1), row(across[1]))
+    return window_x, window_y, depth_weights(base(2), row(across[2]), size)
+
+
+def border_rows(body, cells_x, cells_y):
+    @pl.loop(0, 2)
+    def _(side):
+        body(side * (cells_x - 1), range(cells_y))
+
+    @pl.loop(1, cells_x - 1)
+    def _(row):
+        body(row, (0, cells_y - 1))
+
+
+def inner_rows(body, cells_x, cells_y):
+    @pl.loop(1, cells_x - 1)
+    def _(row):
+        body(row, range(1, cells_y - 1))
 
 
 def depth_forward_kernel(grid_ref, table_ref, out_ref):
@@ -332,22 +326,40 @@
     return copies
 
 
-def fold_kernel(count_x, count_y, in_ref, out_ref, *scratch):
+def spread_kernel(
+    count_x, count_y, charge_ref, fraction_ref, base_ref, out_ref, ext_ref, *scratch
+):
     row_out, row_in, col_out, col_in, edge_out, edge_in, sent, here = scratch
     nx, ny, size = out_ref.shape
+    cells_x, cells_y, slots = charge_ref.shape
+    ext_ref[...] = jnp.zeros_like(ext_ref)
+
+    def work(row, chosen):
+        across = [spline_weights(fraction_ref[dim, row]) for dim in range(3)]
+        charge = charge_ref[row]
+        for cell in chosen:
+            window_x, window_y, depth = cell_tables(across, base_ref, row, cell, size)
+            loaded = charge[cell : cell + 1, :] * window_x
+            lifted = (loaded[:, None, :] * window_y[None, :, :]).reshape(REACH * REACH, slots)
+            patch = dot3(halves(lifted), depth, NT).reshape(REACH, REACH, size)
+            span = (pl.ds(row * CELL, REACH), pl.ds(cell * CELL, REACH), slice(None))
+            ext_ref[span] = ext_ref[span] + patch
+
+    copies = neighbour_copies(count_x, count_y, *scratch)
+    border_rows(work, cells_x, cells_y)
     for i in range(2):
         x = (0, nx + 2)[i]
         y = (0, ny + 2)[i]
-        row_out[i] = in_ref[x : x + 2, 2 : ny + 2, :]
+        row_out[i] = ext_ref[x : x + 2, 2 : ny + 2, :]
         for j in range(2):
-            col_out[i, j] = in_ref[2 : nx + 2, y + j, :]
+            col_out[i, j] = ext_ref[2 : nx + 2, y + j, :]
             edge = (0, ny + 2)[j]
             for k in range(2):
-                edge_out[2 * i + j, 2 * k : 2 * k + 2] = in_ref[x + k, edge : edge + 2, :]
-    copies = neighbour_copies(count_x, count_y, *scratch)
+                edge_out[2 * i + j, 2 * k : 2 * k + 2] = ext_ref[x + k, edge : edge + 2, :]
     for copy in copies:
         copy.start()
-    out_ref[...] = in_ref[2 : nx + 2, 2 : ny + 2, :]
+    inner_rows(work, cells_x, cells_y)
+    out_ref[...] = ext_ref[2 : nx + 2, 2 : ny + 2, :]
     for copy in copies:
         copy.wait()
     for i in range(2):
@@ -363,9 +375,23 @@
                 )
 
 
-def halo_kernel(count_x, count_y, in_ref, out_ref, *scratch):
+def gather_kernel(
+    count_x, count_y, fraction_ref, base_ref, in_ref, out_ref, ext_ref, *scratch
+):
     row_out, row_in, col_out, col_in, edge_out, edge_in, sent, here = scratch
     nx, ny, size = in_ref.shape
+    cells_x, cells_y, slots = out_ref.shape
+
+    def work(row, chosen):
+        across = [spline_weights(fraction_ref[dim, row]) for dim in range(3)]
+        for cell in chosen:
+            window_x, window_y, depth = cell_tables(across, base_ref, row, cell, size)
+            span = (pl.ds(row * CELL, REACH), pl.ds(cell * CELL, REACH), slice(None))
+            window = ext_ref[span].reshape(REACH * REACH, size)
+            value = dot3(halves(window), depth, NN).reshape(REACH, REACH, slots)
+            value = jnp.sum(value * window_x[:, None, :], axis=0) * window_y
+            out_ref[row, cell : cell + 1, :] = jnp.sum(value, axis=0, keepdims=True)
+
     for i in range(2):
         x = (0, nx - 2)[i]
         y = (0, ny - 2)[i]
@@ -378,22 +404,25 @@
     copies = neighbour_copies(count_x, count_y, *scratch)
     for copy in copies:
         copy.start()
-    out_ref[2 : nx + 2, 2 : ny + 2, :] = in_ref[...]
+    ext_ref[2 : nx + 2, 2 : ny + 2, :] = in_ref[...]
+    inner_rows(work, cells_x, cells_y)
     for copy in copies:
         copy.wait()
     for i in range(2):
         x = (nx + 2, 0)[i]
         y = (ny + 2, 0)[i]
-        out_ref[x : x + 2, 2 : ny + 2, :] = row_in[i]
+        ext_ref[x : x + 2, 2 : ny + 2, :] = row_in[i]
         for j in range(2):
-            out_ref[2 : nx + 2, y + j, :] = col_in[i, j]
+            ext_ref[2 : nx + 2, y + j, :] = col_in[i, j]
             edge = (ny + 2, 0)[j]
             for k in range(2):
-                out_ref[x + k, edge : edge + 2, :] = edge_in[2 * i + j, 2 * k : 2 * k + 2]
+                ext_ref[x + k, edge : edge + 2, :] = edge_in[2 * i + j, 2 * k : 2 * k + 2]
+    border_rows(work, cells_x, cells_y)
 
 
 def halo_scratch(nx, ny, size):
     shapes = [(2, 2, ny, size)] * 2 + [(2, 2, nx, size)] * 2 + [(4, 4, size)] * 2
+    shapes = [(nx + 4, ny + 4, size)] + shapes
     return [pltpu.VMEM(shape, jnp.float32) for shape in shapes] + [
         pltpu.SemaphoreType.DMA((8,)),
         pltpu.SemaphoreType.DMA((8,)),
@@ -444,26 +473,13 @@
             vmem_limit_bytes=VMEM_LIMIT, collective_id=number, has_side_effects=True
         )
 
-    whole = lambda *dims: pl.BlockSpec(dims, lambda *_: (0,) * len(dims))
-    atoms = pl.BlockSpec((3, 1, cells_y, slots), lambda i: (0, i, 0, 0))
-    cells = pl.BlockSpec((1, cells_y, slots), lambda i: (i, 0, 0))
-
-    extended = pl.pallas_call(
-        functools.partial(spread_kernel, size),
-        grid=(cells_x,),
-        in_specs=[cells, atoms, atoms],
-        out_specs=whole(local_x + 4, local_y + 4, size),
-        out_shape=jax.ShapeDtypeStruct((local_x + 4, local_y + 4, size), jnp.float32),
-        compiler_params=params,
-        name="spread",
-    )(charge, fraction, grid_base)
     spread = pl.pallas_call(
-        functools.partial(fold_kernel, px_size, py_size),
+        functools.partial(spread_kernel, px_size, py_size),
         out_shape=jax.ShapeDtypeStruct((local_x, local_y, size), jnp.float32),
         scratch_shapes=halo_scratch(local_x, local_y, size),
         compiler_params=linked(0),
-        name="fold",
-    )(extended)
+        name="spread",
+    )(charge, fraction, grid_base)
 
     forward_z, inverse_z = wave_tables(size, devices, 1.0 / (size * full_x * full_y))
     columns = pl.pallas_call(
@@ -506,22 +522,13 @@
         compiler_params=params,
         name="depth_inverse",
     )(returned, halves_np(inverse_z))
-    halo_potential = pl.pallas_call(
-        functools.partial(halo_kernel, px_size, py_size),
-        out_shape=jax.ShapeDtypeStruct(extended.shape, jnp.float32),
+    gradient = pl.pallas_call(
+        functools.partial(gather_kernel, px_size, py_size),
+        out_shape=jax.ShapeDtypeStruct(cotangent.shape, jnp.float32),
         scratch_shapes=halo_scratch(local_x, local_y, size),
         compiler_params=linked(2),
-        name="halo",
-    )(potential)
-    gradient = pl.pallas_call(
-        functools.partial(gather_kernel, size),
-        grid=(cells_x,),
-        in_specs=[atoms, atoms, whole(local_x + 4, local_y + 4, size)],
-        out_specs=cells,
-        out_shape=jax.ShapeDtypeStruct(cotangent.shape, jnp.float32),
-        compiler_params=params,
         name="gather",
-    )(fraction, grid_base, halo_potential)
+    )(fraction, grid_base, potential)
     return jnp.where(occupied, gradient, 0.0)
 
 

time: 156 us -> 140 us (0.90)
  Pallas kernels: 151 us -> 135 us
    pallas_call x4 -> x2, Pallas kernels: 49.5 us -> 35.4 us  [the longest x1 20.2 us: per_device(): pl.pallas_call(functools.partial(spread_kernel, px_size, py_size), out_sh...]
    pallas_call x1, Pallas kernels: 98.3 us -> 96.6 us  [per_device(): pl.pallas_call(functools.partial(exchange_kernel, px_size, py_size), in_s...]
where the time goes in v3:
time: 140 us
  Pallas kernels  135 us (96%)
  local copies, waits for them, and re-layouts  3.23 us (2%)
  other arithmetic  1.64 us (1%)
    pallas_call x1, Pallas kernels, per_device(): pl.pallas_call(functools.partial(exchange_kernel, px_size, py_size), in_s...  96.6 us
    pallas_call x1, Pallas kernels, per_device(): pl.pallas_call(functools.partial(spread_kernel, px_size, py_size), out_sh...  20.2 us
    pallas_call x1, Pallas kernels, per_device(): pl.pallas_call(functools.partial(gather_kernel, px_size, py_size), out_sh...  15.2 us
    unnamed x24, local copies, waits for them, and re-layouts  3.23 us

profile of v3, /device:TPU:0, one launch (start us, length us, event | category | flops | bytes accessed | tf_op | source)
XLA Modules:
  0.0 140.0 jit_solution(11807109866763208729)
XLA Ops:
  0.0 0.9 fusion.1.charge_ref
  0.9 0.0 copy-start.1
  0.9 0.9 copy-done.1
  1.9 0.0 copy-start.3
  1.9 0.9 copy-done.3
  2.8 0.0 copy-start.9
  2.8 20.2 %spread.1.grid_ref = f32[32,64,256]{2,1,0:T(8,128)S(1)} custom-call(f32[8,16,128]{2,1,0:T(8,128)S(1)} %fusion.1.charge_ref, f32[3,8,16,128]{3,2,1,0:T(8,128)S(1)} %copy-done.1, s32[3,8,16,128]{3,2,1,0:T(8,128)S(1)} %copy-done.3), custom_call_target="tpu_custom_call" | custom-call | tf_op jit(solution)/shard_map/spread/pallas_call | solution.py:476
  23.0 0.0 copy-done.9
  23.0 0.0 copy-start.5
  23.0 0.0 copy-start.6
  23.0 0.0 copy-start.7
  23.0 0.0 copy-start.8
  23.0 1.9 %depth_forward.1 = f32[4096,128]{1,0:T(8,128)S(1)} custom-call(f32[32,64,256]{2,1,0:T(8,128)S(1)} %spread.1.grid_ref, bf16[2,256,256]{2,1,0:T(8,128)(2,1)S(1)} %copy-done.9), custom_call_target="tpu_custom_call" | custom-call | tf_op jit(solution)/shard_map/depth_forward/pallas_call | solution.py:485
  24.9 0.0 copy-start
  24.9 1.3 copy-done
  26.2 0.0 copy-done.5
  26.2 0.0 copy-done.6
  26.2 0.0 copy-done.7
  26.2 0.0 copy-done.8
  26.2 0.0 copy-start.10
  26.3 96.6 %exchange.1 = f32[32,4,2,16,128]{4,3,2,1,0:T(8,128)S(1)} custom-call(f32[32,4,2,16,128]{4,3,2,1,0:T(8,128)} %bitcast.2, f32[8,256,256]{2,1,0:T(8,128)} %influence_ref.1, bf16[2,256,512]{2,1,0:T(8,128)(2,1)S(1)} %copy-done.8, bf16[2,256,512]{2,1,0:T(8,128)(2,1)S(1)} %copy-done.7, bf16[2,512,256]{2,1,0:T(8,128)(2,1)S(1)} %copy-done.6, ...), custom_call_target="tpu_custom_call" | custom-call | tf_op jit(solution)/shard_map/exchange/pallas_call | solution.py:501
  122.9 0.0 copy-done.10
  122.9 0.0 copy-start.2
  122.9 0.0 copy-start.4
  122.9 1.1 depth_inverse.1.in_ref
  124.0 0.0 copy-done.2
  124.0 0.0 copy-done.4
  124.0 0.0 copy-start.11
  124.1 15.2 %gather.1 = f32[8,16,128]{2,1,0:T(8,128)S(1)} custom-call(f32[3,8,16,128]{3,2,1,0:T(8,128)S(1)} %copy-done.2, s32[3,8,16,128]{3,2,1,0:T(8,128)S(1)} %copy-done.4, f32[32,64,256]{2,1,0:T(8,128)S(1)} %depth_inverse.1.in_ref), custom_call_target="tpu_custom_call" | custom-call | tf_op jit(solution)/shard_map/gather/pallas_call | solution.py:525
  139.3 0.0 copy-done.11
  139.3 0.7 fusion
Async XLA Ops:
  0.9 0.9 copy-start.1
  1.9 0.9 copy-start.3
  2.8 20.2 %copy-start.9 = (bf16[2,256,256]{2,1,0:T(8,128)(2,1)S(1)}, bf16[2,256,256]{2,1,0:T(8,128)(2,1)}, u32[]{:S(2)}) copy-start(bf16[2,256,256]{2,1,0:T(8,128)(2,1)} %constant.14.clone.table_ref) | copy-start | bytes 786436
  23.0 3.3 %copy-start.5 = (bf16[2,512,256]{2,1,0:T(8,128)(2,1)S(1)}, bf16[2,512,256]{2,1,0:T(8,128)(2,1)}, u32[]{:S(2)}) copy-start(bf16[2,512,256]{2,1,0:T(8,128)(2,1)} %constant.18.clone.left_back_ref) | copy-start | bytes 1572868
  23.0 3.3 %copy-start.6 = (bf16[2,512,256]{2,1,0:T(8,128)(2,1)S(1)}, bf16[2,512,256]{2,1,0:T(8,128)(2,1)}, u32[]{:S(2)}) copy-start(bf16[2,512,256]{2,1,0:T(8,128)(2,1)} %constant.17.clone.left_ref) | copy-start | bytes 1572868
  23.0 3.3 %copy-start.7 = (bf16[2,256,512]{2,1,0:T(8,128)(2,1)S(1)}, bf16[2,256,512]{2,1,0:T(8,128)(2,1)}, u32[]{:S(2)}) copy-start(bf16[2,256,512]{2,1,0:T(8,128)(2,1)} %constant.16.clone.back_ref) | copy-start | bytes 1572868
  23.0 3.2 %copy-start.8 = (bf16[2,256,512]{2,1,0:T(8,128)(2,1)S(1)}, bf16[2,256,512]{2,1,0:T(8,128)(2,1)}, u32[]{:S(2)}) copy-start(bf16[2,256,512]{2,1,0:T(8,128)(2,1)} %constant.15.clone.right_ref) | copy-start | bytes 1572868
  24.9 1.3 copy-start
  26.2 96.6 %copy-start.10 = (bf16[2,256,256]{2,1,0:T(8,128)(2,1)S(1)}, bf16[2,256,256]{2,1,0:T(8,128)(2,1)}, u32[]{:S(2)}) copy-start(bf16[2,256,256]{2,1,0:T(8,128)(2,1)} %constant.19.clone.table_ref) | copy-start | bytes 786436
  122.9 1.1 copy-start.2
  122.9 1.1 copy-start.4
  124.0 15.2 %copy-start.11 = (s32[8,16]{1,0:T(8,128)S(1)}, s32[8,16]{1,0:T(8,128)}, u32[]{:S(2)}) copy-start(s32[8,16]{1,0:T(8,128)} %param.14) | copy-start | bytes 1540

commit v4 on v3

--- a/solution.py
+++ b/solution.py
@@ -32,7 +32,9 @@
     def one(a, b):
         return lax.dot_general(a, b, (dims, ((), ())), preferred_element_type=jnp.float32)
 
-    return one(left[0], right[0]) + (one(left[0], right[1]) + one(left[1], right[0]))
+    rows = left[0].shape[0]
+    both = one(jnp.concatenate(left, axis=0), right[0])
+    return both[:rows] + (one(left[0], right[1]) + both[rows:])
 
 
 NN = ((1,), (0,))

time: 140 us -> 138 us (0.986)
  Pallas kernels: 135 us -> 133 us
where the time goes in v4:
time: 138 us
  Pallas kernels  133 us (96%)
  local copies, waits for them, and re-layouts  3.23 us (2%)
  other arithmetic  1.64 us (1%)
    pallas_call x1, Pallas kernels, per_device(): pl.pallas_call(functools.partial(exchange_kernel, px_size, py_size), in_s...  96.6 us
    pallas_call x1, Pallas kernels, per_device(): pl.pallas_call(functools.partial(spread_kernel, px_size, py_size), out_sh...  19.1 us
    pallas_call x1, Pallas kernels, per_device(): pl.pallas_call(functools.partial(gather_kernel, px_size, py_size), out_sh...  14.4 us
    unnamed x24, local copies, waits for them, and re-layouts  3.23 us

profile of v4, /device:TPU:0, one launch (start us, length us, event | category | flops | bytes accessed | tf_op | source)
XLA Modules:
  0.0 138.1 jit_solution(10464151698815461671)
XLA Ops:
  0.0 0.9 fusion.1.charge_ref
  0.9 0.0 copy-start.1
  0.9 0.9 copy-done.1
  1.9 0.0 copy-start.3
  1.9 0.9 copy-done.3
  2.8 0.0 copy-start.9
  2.8 19.1 %spread.1.grid_ref = f32[32,64,256]{2,1,0:T(8,128)S(1)} custom-call(f32[8,16,128]{2,1,0:T(8,128)S(1)} %fusion.1.charge_ref, f32[3,8,16,128]{3,2,1,0:T(8,128)S(1)} %copy-done.1, s32[3,8,16,128]{3,2,1,0:T(8,128)S(1)} %copy-done.3), custom_call_target="tpu_custom_call" | custom-call | tf_op jit(solution)/shard_map/spread/pallas_call | solution.py:478
  21.9 0.0 copy-done.9
  21.9 0.0 copy-start.5
  21.9 0.0 copy-start.6
  22.0 0.0 copy-start.7
  22.0 0.0 copy-start.8
  22.0 1.8 %depth_forward.1 = f32[4096,128]{1,0:T(8,128)S(1)} custom-call(f32[32,64,256]{2,1,0:T(8,128)S(1)} %spread.1.grid_ref, bf16[2,256,256]{2,1,0:T(8,128)(2,1)S(1)} %copy-done.9), custom_call_target="tpu_custom_call" | custom-call | tf_op jit(solution)/shard_map/depth_forward/pallas_call | solution.py:487
  23.8 0.0 copy-start
  23.8 1.3 copy-done
  25.2 0.0 copy-done.5
  25.2 0.0 copy-done.6
  25.2 0.0 copy-done.7
  25.2 0.0 copy-done.8
  25.2 0.0 copy-start.10
  25.2 96.6 %exchange.1 = f32[32,4,2,16,128]{4,3,2,1,0:T(8,128)S(1)} custom-call(f32[32,4,2,16,128]{4,3,2,1,0:T(8,128)} %bitcast.2, f32[8,256,256]{2,1,0:T(8,128)} %influence_ref.1, bf16[2,256,512]{2,1,0:T(8,128)(2,1)S(1)} %copy-done.8, bf16[2,256,512]{2,1,0:T(8,128)(2,1)S(1)} %copy-done.7, bf16[2,512,256]{2,1,0:T(8,128)(2,1)S(1)} %copy-done.6, ...), custom_call_target="tpu_custom_call" | custom-call | tf_op jit(solution)/shard_map/exchange/pallas_call | solution.py:503
  121.8 0.0 copy-done.10
  121.8 0.0 copy-start.2
  121.8 0.0 copy-start.4
  121.8 1.1 depth_inverse.1.in_ref
  123.0 0.0 copy-done.2
  123.0 0.0 copy-done.4
  123.0 0.0 copy-start.11
  123.0 14.4 %gather.1 = f32[8,16,128]{2,1,0:T(8,128)S(1)} custom-call(f32[3,8,16,128]{3,2,1,0:T(8,128)S(1)} %copy-done.2, s32[3,8,16,128]{3,2,1,0:T(8,128)S(1)} %copy-done.4, f32[32,64,256]{2,1,0:T(8,128)S(1)} %depth_inverse.1.in_ref), custom_call_target="tpu_custom_call" | custom-call | tf_op jit(solution)/shard_map/gather/pallas_call | solution.py:527
  137.4 0.0 copy-done.11
  137.4 0.7 fusion
Async XLA Ops:
  0.9 0.9 copy-start.1
  1.9 0.9 copy-start.3
  2.8 19.1 %copy-start.9 = (bf16[2,256,256]{2,1,0:T(8,128)(2,1)S(1)}, bf16[2,256,256]{2,1,0:T(8,128)(2,1)}, u32[]{:S(2)}) copy-start(bf16[2,256,256]{2,1,0:T(8,128)(2,1)} %constant.14.clone.table_ref) | copy-start | bytes 786436
  21.9 3.2 %copy-start.5 = (bf16[2,512,256]{2,1,0:T(8,128)(2,1)S(1)}, bf16[2,512,256]{2,1,0:T(8,128)(2,1)}, u32[]{:S(2)}) copy-start(bf16[2,512,256]{2,1,0:T(8,128)(2,1)} %constant.18.clone.left_back_ref) | copy-start | bytes 1572868
  21.9 3.2 %copy-start.6 = (bf16[2,512,256]{2,1,0:T(8,128)(2,1)S(1)}, bf16[2,512,256]{2,1,0:T(8,128)(2,1)}, u32[]{:S(2)}) copy-start(bf16[2,512,256]{2,1,0:T(8,128)(2,1)} %constant.17.clone.left_ref) | copy-start | bytes 1572868
  22.0 3.2 %copy-start.7 = (bf16[2,256,512]{2,1,0:T(8,128)(2,1)S(1)}, bf16[2,256,512]{2,1,0:T(8,128)(2,1)}, u32[]{:S(2)}) copy-start(bf16[2,256,512]{2,1,0:T(8,128)(2,1)} %constant.16.clone.back_ref) | copy-start | bytes 1572868
  22.0 3.2 %copy-start.8 = (bf16[2,256,512]{2,1,0:T(8,128)(2,1)S(1)}, bf16[2,256,512]{2,1,0:T(8,128)(2,1)}, u32[]{:S(2)}) copy-start(bf16[2,256,512]{2,1,0:T(8,128)(2,1)} %constant.15.clone.right_ref) | copy-start | bytes 1572868
  23.8 1.3 copy-start
  25.2 96.6 %copy-start.10 = (bf16[2,256,256]{2,1,0:T(8,128)(2,1)S(1)}, bf16[2,256,256]{2,1,0:T(8,128)(2,1)}, u32[]{:S(2)}) copy-start(bf16[2,256,256]{2,1,0:T(8,128)(2,1)} %constant.19.clone.table_ref) | copy-start | bytes 786436
  121.8 1.2 copy-start.2
  121.8 1.2 copy-start.4
  123.0 14.4 %copy-start.11 = (s32[8,16]{1,0:T(8,128)S(1)}, s32[8,16]{1,0:T(8,128)}, u32[]{:S(2)}) copy-start(s32[8,16]{1,0:T(8,128)} %param.14) | copy-start | bytes 1540
